TPU v7x, 32 devices: a whole 2x2x4 slice. The times are simulated.
32 devices in a mesh: blk: 4 (over y, x), grp: 8 (over z, core).
Axes of the slice: x: 2, y: 2, z: 4, core: 2. Of those that a mesh axis runs over, the one named last changes fastest.
Arguments:
- amplitudes: bfloat16 [256, 6144], P(('blk', 'grp')), may hold values from -6 to 6
- integrals: bfloat16 [6144, 512], P('grp', 'blk'), may hold values from -0.109375 to 0.109375
- tile_mask: int32 [32, 48], P(('blk', 'grp')), may hold values from 0 to 1, as said below
- tile_size: int32 [48], replicated, may hold values from 64 to 128, as said below
Outputs:
- ladder: bfloat16 [256, 512], P(('blk', 'grp'))
Inputs may be any that keep to these rules, and one draw needn't show every extreme that they name: `tile_mask`: mask entries are 0 or 1; domains differ in how many of their tiles are live. `tile_size`: one tile is full and one is half full.
All inputs are finite; a program needn't handle non-finite values.
Results may differ from a plain program's by a relative error of at most 0.001.
Values may be sent and summed in bfloat16 or wider, within the bound.
No kernel may reach another device: no remote copies, remote signals or barrier semaphores. Data moves between devices by JAX's collectives and lax.ppermute only.
A program may use at most 64 MiB of HBM per device.

v0:
```python
import jax
import jax.numpy as jnp
from jax import lax
from jax.sharding import PartitionSpec as P


def body(amplitudes, integrals, tile_mask, tile_size):
    row_count, width = amplitudes.shape
    tile_count = tile_size.shape[0]
    tile_width = width // tile_count
    lane_index = lax.broadcasted_iota(jnp.int32, (tile_count, tile_width), 1)
    live_tiles = (tile_mask[0][:, None] == 1) & (lane_index < tile_size[:, None])
    shaped = amplitudes.reshape(row_count, tile_count, tile_width)
    masked = jnp.where(live_tiles[None], shaped, jnp.zeros_like(shaped)).reshape(row_count, width)
    regrouped = lax.all_to_all(masked, "grp", split_axis=1, concat_axis=0, tiled=True)
    partial_value = jnp.dot(
        regrouped,
        lax.all_gather(integrals, "blk", axis=1, tiled=True),
        preferred_element_type=jnp.float32,
    )
    ladder = lax.psum_scatter(partial_value, "grp", scatter_dimension=0, tiled=True)
    return ladder.astype(jnp.bfloat16)


def solution(mesh):
    return jax.shard_map(
        body,
        mesh=mesh,
        in_specs=(P(("blk", "grp"), None), P("grp", "blk"), P(("blk", "grp"), None), P()),
        out_specs=P(("blk", "grp"), None),
        check_vma=False,
    )
```

profile of v0, /device:TPU:0, one launch (start us, length us, event | category | flops | bytes accessed | tf_op | source)
XLA Modules:
  0.0 67.3 jit_solution(13664911008152616803)
XLA Ops:
  6.5 0.0 copy-start.1
  6.5 0.7 compare_bitcast_fusion
  7.2 0.0 copy-done.1
  7.2 0.1 lt.14
  7.3 0.1 fusion.2
  7.4 0.0 copy-start
  7.4 1.6 %broadcast_select_fusion = bf16[8,6144]{1,0:T(8,128)(2,1)} fusion(bf16[8,6144]{1,0:T(8,128)(2,1)} %param.4, pred[6144]{0:T(1024)(128)(4,1)S(1)} %fusion.2), kind=kLoop, calls=%fused_computation.2 | loop fusion | flops 49152 | bytes 202752 | tf_op jit(solution)/shard_map/jit(_where)/select_n | solution.py:14
  9.0 6.3 %all-to-all-start = ((bf16[8,8,768]{2,0,1:T(8,128)(2,1)}), bf16[8,8,768]{2,0,1:T(8,128)(2,1)S(1)}, u32[]{:S(2)}, u32[]{:S(2)}) async-start(bf16[8,8,768]{2,0,1:T(8,128)(2,1)} %bitcast.4), calls=%async_computation | async-start | bytes 196608 | tf_op jit(solution)/shard_map/all_to_all | solution.py:15
  15.3 0.0 reduce-scatter.2.cloned.1.call-start
  15.4 0.0 copy-done
  15.4 12.7 %all_gather.3 = bf16[768,512]{1,0:T(8,128)(2,1)S(1)} all-gather(bf16[768,128]{1,0:T(8,128)(2,1)S(1)} %copy-done), channel_id=1, replica_groups=mesh['blk'=4,'grp'=8] {'blk'}, dimensions={1}, use_global_device_ids=true | all-gather | bytes 983040 | tf_op jit(solution)/shard_map/all_gather | solution.py:18
  28.1 0.0 all-to-all-done
  28.1 0.9 %fusion = f32[64,512]{1,0:T(8,128)} fusion(bf16[768,512]{1,0:T(8,128)(2,1)S(1)} %all_gather.3, bf16[8,8,768]{2,0,1:T(8,128)(2,1)S(1)} %all-to-all-done), kind=kOutput, calls=%fused_computation | convolution fusion | flops 50331648 | bytes 1015808 | tf_op jit(solution)/shard_map/dot_general | solution.py:16
  29.0 0.0 reduce-scatter.2.cloned.1.call-update
  29.1 30.1 %reduce-scatter.2.cloned.1.call-done = f32[8,512]{1,0:T(8,128)} async-done(((f32[64,512]{1,0:T(8,128)}), f32[8,512]{1,0:T(8,128)}) %reduce-scatter.2.cloned.1.call-update) | async-done | bytes 16400 | tf_op jit(solution)/shard_map/reduce_scatter | solution.py:21
  59.2 1.3 %convert_element_type.3 = bf16[8,512]{1,0:T(8,128)(2,1)} convert(f32[8,512]{1,0:T(8,128)} %reduce-scatter.2.cloned.1.call-done) | non-fusion elementwise | flops 4096 | bytes 24576 | tf_op jit(solution)/shard_map/convert_element_type | solution.py:22
Async XLA Ops:
  6.5 0.7 %copy-start.1 = (s32[48]{0:T(128)S(1)}, s32[48]{0:T(128)}, u32[]{:S(2)}) copy-start(s32[48]{0:T(128)} %param.7) | copy-start | bytes 580
  7.4 8.0 %copy-start = (bf16[768,128]{1,0:T(8,128)(2,1)S(1)}, bf16[768,128]{1,0:T(8,128)(2,1)}, u32[]{:S(2)}) copy-start(bf16[768,128]{1,0:T(8,128)(2,1)} %param.5) | copy-start | bytes 589828
  9.0 19.1 %all-to-all-start = ((bf16[8,8,768]{2,0,1:T(8,128)(2,1)}), bf16[8,8,768]{2,0,1:T(8,128)(2,1)S(1)}, u32[]{:S(2)}, u32[]{:S(2)}) async-start(bf16[8,8,768]{2,0,1:T(8,128)(2,1)} %bitcast.4), calls=%async_computation | async-start | bytes 196608 | tf_op jit(solution)/shard_map/all_to_all | solution.py:15
  15.3 43.8 %reduce-scatter.2.cloned.1.call-start = ((), (), s32[]{:S(2)}) async-start(), calls=%async_computation.2 | async-start | bytes 147456 | tf_op jit(solution)/shard_map/reduce_scatter | solution.py:21
Sparse Core Ops, SparseCore 0:
  29.2 29.9 reduce-scatter.1
where the time goes:
time: 67.7 us; the launch traced here: 67.3 us
  waiting for transfers between devices  30.1 us (44%)
  between operations  13.4 us (20%)
  blocking collectives  12.7 us (19%)
  starting transfers between devices  6.36 us (9%)
  other arithmetic  3.67 us (5%)
  matrix products  0.91 us (1%)
    reduce_scatter x1, waiting for transfers between devices, body(): lax.psum_scatter(partial_value, 'grp', scatter_dimension=0, tiled=True)  30.1 us
    all_gather x1, blocking collectives, body(): lax.all_gather(integrals, 'blk', axis=1, tiled=True)  12.7 us
    all_to_all x1, starting transfers between devices, body(): lax.all_to_all(masked, 'grp', split_axis=1, concat_axis=0, tiled=True)  6.33 us
    select_n x1, other arithmetic, body(): jnp.where(live_tiles[None], shaped, jnp.zeros_like(shaped))  1.61 us
  transfers between devices with their start and end apart: 2, of which 1 were waited for; matrix products, arithmetic and copies ran while one was open for 0% of the time, Pallas kernels for 0%

commit v1 on v0

v1 whole, which is shorter than its diff:
```python
import functools

import jax
import jax.numpy as jnp
from jax import lax
from jax.experimental import pallas as pl
from jax.experimental.pallas import tpu as pltpu
from jax.sharding import PartitionSpec as P

CORES = 2
VMEM = pl.BlockSpec(memory_space=pltpu.VMEM)
SMEM = pl.BlockSpec(memory_space=pltpu.SMEM)


def mask_kernel(order, mask_ref, size_ref, amplitude_ref, *out_refs):
    grp = lax.axis_index("grp")
    chip, core = grp // CORES, lax.rem(grp, CORES)
    rows, width = amplitude_ref.shape
    tile = width // size_ref.shape[0]
    tiles = out_refs[0].shape[1] // tile // CORES
    lane = lax.broadcasted_iota(jnp.int32, (rows, tile), 1)
    for out_ref, step in zip(out_refs, order):
        for half in range(CORES):
            first = ((chip ^ step) * CORES + (core ^ half)) * tiles
            for t in range(tiles):
                k = first + t
                live = jnp.where(mask_ref[0, k] == 1, size_ref[k], 0)
                value = amplitude_ref[:, pl.ds(pl.multiple_of(k * tile, tile), tile)]
                place = (half * tiles + t) * tile
                out_ref[:, place : place + tile] = jnp.where(lane < live, value, jnp.zeros_like(value))


def live_blocks(amplitudes, tile_mask, tile_size, order, members):
    rows, width = amplitudes.shape
    shape = jax.ShapeDtypeStruct((rows, CORES * width // members), amplitudes.dtype)
    return pl.pallas_call(
        functools.partial(mask_kernel, order),
        out_shape=[shape] * len(order),
        in_specs=[SMEM, SMEM, VMEM],
        out_specs=[VMEM] * len(order),
        name="live_blocks",
    )(tile_mask, tile_size, amplitudes)


def body(blk_size, grp_size, amplitudes, integrals, tile_mask, tile_size):
    rows, depth, cols = amplitudes.shape[0], *integrals.shape
    chips = grp_size // CORES
    order = tuple(range(chips - 1, 0, -1))
    blk = lax.axis_index("blk")

    def between(array, axis, size, step):
        return lax.ppermute(array, axis, [(k, k ^ step) for k in range(size)])

    own = jnp.concatenate(
        [integrals] + [between(integrals, "blk", blk_size, step) for step in range(1, blk_size)], axis=1
    )
    blocks = live_blocks(amplitudes, tile_mask, tile_size, (0,) + order, grp_size)
    received = [between(b, "grp", grp_size, CORES * step) for b, step in zip(blocks[1:], order)]
    received[-1], own = lax.optimization_barrier((received[-1], own))
    other = between(own, "grp", grp_size, 1)
    live = jnp.concatenate([blocks[0]] + received, axis=0)
    partial = jnp.dot(live[:, :depth], own, preferred_element_type=jnp.float32)
    partial += jnp.dot(live[:, depth:], other, preferred_element_type=jnp.float32)
    ladder = partial[:rows]
    for place, step in enumerate(order, 1):
        ladder += between(partial[place * rows : (place + 1) * rows], "grp", grp_size, CORES * step)
    ladder = ladder.astype(jnp.bfloat16)
    pieces = [ladder[:, k * cols : (k + 1) * cols] for k in range(blk_size)]
    return jnp.concatenate([lax.select_n(blk ^ k, *pieces) for k in range(blk_size)], axis=1)


def solution(mesh):
    return jax.shard_map(
        functools.partial(body, mesh.shape["blk"], mesh.shape["grp"]),
        mesh=mesh,
        in_specs=(P(("blk", "grp"), None), P("grp", "blk"), P(("blk", "grp"), None), P()),
        out_specs=P(("blk", "grp"), None),
        check_vma=False,
    )
```

time: 67.7 us -> 26.7 us (0.39)
  waiting for transfers between devices: 30.1 us -> 8.78 us
  between operations: 13.4 us -> 0.09 us
  blocking collectives: 12.7 us -> 0 us
  starting transfers between devices: 6.36 us -> 13.9 us
  other arithmetic: 3.67 us -> 1.64 us
  Pallas kernels: 0 us -> 1.68 us
    reduce_scatter x1 -> x0, waiting for transfers between devices: 30.1 us -> none  [body(): lax.psum_scatter(partial_value, 'grp', scatter_dimension=0, tiled=True)]
    ppermute x0 -> x10, starting transfers between devices: none -> 13.9 us  [between(): return lax.ppermute(array, axis, [(k, k ^ step) for k in range(size)])]
    all_gather x1 -> x0, blocking collectives: 12.7 us -> none  [body(): lax.all_gather(integrals, 'blk', axis=1, tiled=True)]
    ppermute x0 -> x10, waiting for transfers between devices: none -> 8.78 us  [between(): return lax.ppermute(array, axis, [(k, k ^ step) for k in range(size)])]
    all_to_all x1 -> x0, starting transfers between devices: 6.33 us -> none  [body(): lax.all_to_all(masked, 'grp', split_axis=1, concat_axis=0, tiled=True)]
    pallas_call x0 -> x1, Pallas kernels: none -> 1.68 us  [live_blocks(): pl.pallas_call(functools.partial(mask_kernel, order), out_shape=[shape] *...]
    concatenate x0 -> x2, other arithmetic: none -> 1.62 us  [the longest x1 1.01 us: body(): jnp.concatenate([integrals] + [between(integrals, 'blk', blk_size, step)...]
    select_n x1 -> x2, other arithmetic: 1.61 us -> 0.02 us  [body(): lax.select_n(blk ^ k, *pieces)]
  transfers between devices with their start and end apart: 2 -> 10, of which waited for: 1 -> 5; matrix products, arithmetic and copies ran while one was open for 0% -> 4% of each run, Pallas kernels for 0% -> 6%
where the time goes in v1:
time: 26.7 us; the launch traced here: 26.6 us
  starting transfers between devices  13.9 us (52%)
  waiting for transfers between devices  8.78 us (33%)
  Pallas kernels  1.68 us (6%)
  other arithmetic  1.64 us (6%)
  matrix products  0.47 us (2%)
    ppermute x10, starting transfers between devices, between(): return lax.ppermute(array, axis, [(k, k ^ step) for k in range(size)])  13.9 us
    ppermute x10, waiting for transfers between devices, between(): return lax.ppermute(array, axis, [(k, k ^ step) for k in range(size)])  8.78 us
    pallas_call x1, Pallas kernels, live_blocks(): pl.pallas_call(functools.partial(mask_kernel, order), out_shape=[shape] *...  1.68 us
    concatenate x1, other arithmetic, body(): jnp.concatenate([integrals] + [between(integrals, 'blk', blk_size, step)...  1.01 us
    concatenate x1, other arithmetic, body(): jnp.concatenate([lax.select_n(blk ^ k, *pieces) for k in range(blk_size)]...  0.6 us
  transfers between devices with their start and end apart: 10, of which 5 were waited for; matrix products, arithmetic and copies ran while one was open for 4% of the time, Pallas kernels for 6%

profile of v1, /device:TPU:0, one launch (start us, length us, event | category | flops | bytes accessed | tf_op | source)
XLA Modules:
  0.0 26.6 jit_solution(7923919141197748712)
XLA Ops:
  0.0 2.9 %collective-permute-start.3 = (bf16[768,128]{1,0:T(8,128)(2,1)}, bf16[768,128]{1,0:T(8,128)(2,1)S(1)}, u32[]{:S(2)}, u32[]{:S(2)}) collective-permute-start(bf16[768,128]{1,0:T(8,128)(2,1)} %param.5), channel_id=1, source_target_pairs={{0,8},{8,0},{16,24},{24,16},{1,9},{9,1},{17,25},{25,17},{2,10},{10... | collective-permute-start | bytes 589832 | tf_op jit(solution)/shard_map/ppermute | solution.py:52
  2.9 1.5 %collective-permute-start.4 = (bf16[768,128]{1,0:T(8,128)(2,1)}, bf16[768,128]{1,0:T(8,128)(2,1)S(1)}, u32[]{:S(2)}, u32[]{:S(2)}) collective-permute-start(bf16[768,128]{1,0:T(8,128)(2,1)} %param.5), channel_id=1, source_target_pairs={{0,16},{8,24},{16,0},{24,8},{1,17},{9,25},{17,1},{25,9},{2,18},{10... | collective-permute-start | bytes 589832 | tf_op jit(solution)/shard_map/ppermute | solution.py:52
  4.5 0.0 collective-permute-start.5
  4.5 1.7 %live_blocks.1 = (bf16[8,1536]{1,0:T(8,128)(2,1)}, bf16[8,1536]{1,0:T(8,128)(2,1)}, bf16[8,1536]{1,0:T(8,128)(2,1)}, bf16[8,1536]{1,0:T(8,128)(2,1)}) custom-call(s32[1,48]{1,0:T(1,128)} %mask_ref.1, s32[48]{0:T(128)} %size_ref.1, bf16[8,6144]{1,0:T(8,128)(2,1)} %amplitude_ref.1), custom_call_target="tpu_custom_call" | custom-call | tf_op jit(solution)/shard_map/live_blocks/pallas_call | solution.py:36
  6.1 4.1 %collective-permute-start = (bf16[8,1536]{1,0:T(8,128)(2,1)}, bf16[8,1536]{1,0:T(8,128)(2,1)S(1)}, u32[]{:S(2)}, u32[]{:S(2)}) collective-permute-start(bf16[8,1536]{1,0:T(8,128)(2,1)} %get-tuple-element.12), channel_id=1, source_target_pairs={{0,6},{1,7},{2,4},{3,5},{4,2},{5,3},{6,0},{7,1},{8,14},{9,15},{10,... | collective-permute-start | bytes 73736 | tf_op jit(solution)/shard_map/ppermute | solution.py:52
  10.2 0.0 collective-permute-start.1
  10.2 0.0 collective-permute-done.3
  10.2 0.0 copy-start
  10.2 0.8 %collective-permute-start.2 = (bf16[8,1536]{1,0:T(8,128)(2,1)}, bf16[8,1536]{1,0:T(8,128)(2,1)S(1)}, u32[]{:S(2)}, u32[]{:S(2)}) collective-permute-start(bf16[8,1536]{1,0:T(8,128)(2,1)} %get-tuple-element.14), channel_id=1, source_target_pairs={{0,2},{1,3},{2,0},{3,1},{4,6},{5,7},{6,4},{7,5},{8,10},{9,11},{10,... | collective-permute-start | bytes 73736 | tf_op jit(solution)/shard_map/ppermute | solution.py:52
  11.0 2.7 %collective-permute-done.4 = bf16[768,128]{1,0:T(8,128)(2,1)S(1)} collective-permute-done((bf16[768,128]{1,0:T(8,128)(2,1)}, bf16[768,128]{1,0:T(8,128)(2,1)S(1)}, u32[]{:S(2)}, u32[]{:S(2)}) %collective-permute-start.4) | collective-permute-done | bytes 196640 | tf_op jit(solution)/shard_map/ppermute | solution.py:52
  13.7 0.0 collective-permute-done.5
  13.7 1.0 %pad_maximum_fusion = bf16[768,512]{1,0:T(8,128)(2,1)S(1)} fusion(bf16[768,128]{1,0:T(8,128)(2,1)S(1)} %collective-permute-done.5, bf16[768,128]{1,0:T(8,128)(2,1)S(1)} %collective-permute-done.4, bf16[768,128]{1,0:T(8,128)(2,1)S(1)} %collective-permute-done.3, bf16[768,128]{1,0:T(8,128)(2,1)} %param.5), kind=kLoop, calls=%fused_computation.1 | loop fusion | flops 3145728 | bytes 1572864 | tf_op jit(solution)/shard_map/concatenate | solution.py:54
  14.7 0.0 collective-permute-done.2
  14.8 0.1 collective-permute-start.6
  14.8 0.0 copy-done
  14.9 0.0 collective-permute-done
  14.9 0.3 %collective-permute-done.1 = bf16[8,1536]{1,0:T(8,128)(2,1)S(1)} collective-permute-done((bf16[8,1536]{1,0:T(8,128)(2,1)}, bf16[8,1536]{1,0:T(8,128)(2,1)S(1)}, u32[]{:S(2)}, u32[]{:S(2)}) %collective-permute-start.1) | collective-permute-done | bytes 24608 | tf_op jit(solution)/shard_map/ppermute | solution.py:52
  15.2 1.9 %collective-permute-done.6 = bf16[768,512]{1,0:T(8,128)(2,1)S(1)} collective-permute-done((bf16[768,512]{1,0:T(8,128)(2,1)S(1)}, bf16[768,512]{1,0:T(8,128)(2,1)S(1)}, u32[]{:S(2)}, u32[]{:S(2)}) %collective-permute-start.6) | collective-permute-done | bytes 786464 | tf_op jit(solution)/shard_map/ppermute | solution.py:52
  17.1 0.2 fusion
  17.3 0.2 convolution_add_fusion
  17.6 3.7 %collective-permute-start.7 = (f32[8,512]{1,0:T(8,128)S(1)}, f32[8,512]{1,0:T(8,128)S(1)}, u32[]{:S(2)}, u32[]{:S(2)}) collective-permute-start(f32[8,512]{1,0:T(8,128)S(1)} %get-tuple-element.17), channel_id=1, source_target_pairs={{0,6},{1,7},{2,4},{3,5},{4,2},{5,3},{6,0},{7,1},{8,14},{9,15},{10,... | collective-permute-start | bytes 49160 | tf_op jit(solution)/shard_map/ppermute | solution.py:52
  21.3 0.0 collective-permute-start.8
  21.3 0.8 %collective-permute-start.9 = (f32[8,512]{1,0:T(8,128)S(1)}, f32[8,512]{1,0:T(8,128)S(1)}, u32[]{:S(2)}, u32[]{:S(2)}) collective-permute-start(f32[8,512]{1,0:T(8,128)S(1)} %get-tuple-element.18), channel_id=1, source_target_pairs={{0,2},{1,3},{2,0},{3,1},{4,6},{5,7},{6,4},{7,5},{8,10},{9,11},{10,... | collective-permute-start | bytes 49160 | tf_op jit(solution)/shard_map/ppermute | solution.py:52
  22.1 1.1 %collective-permute-done.7 = f32[8,512]{1,0:T(8,128)S(1)} collective-permute-done((f32[8,512]{1,0:T(8,128)S(1)}, f32[8,512]{1,0:T(8,128)S(1)}, u32[]{:S(2)}, u32[]{:S(2)}) %collective-permute-start.7) | collective-permute-done | bytes 16416 | tf_op jit(solution)/shard_map/ppermute | solution.py:52
  23.2 2.7 %collective-permute-done.8 = f32[8,512]{1,0:T(8,128)S(1)} collective-permute-done((f32[8,512]{1,0:T(8,128)S(1)}, f32[8,512]{1,0:T(8,128)S(1)}, u32[]{:S(2)}, u32[]{:S(2)}) %collective-permute-start.8) | collective-permute-done | bytes 16416 | tf_op jit(solution)/shard_map/ppermute | solution.py:52
  25.9 0.0 collective-permute-done.9
  26.0 0.6 %pad_maximum_fusion.1 = bf16[8,512]{1,0:T(8,128)(2,1)} fusion(bf16[8,128]{1,0:T(8,128)(2,1)S(1)} %get-tuple-element.23, bf16[8,128]{1,0:T(8,128)(2,1)S(1)} %get-tuple-element.22, bf16[8,128]{1,0:T(8,128)(2,1)S(1)} %get-tuple-element.21, bf16[8,128]{1,0:T(8,128)(2,1)S(1)} %get-tuple-element.20), kind=kLoop, calls=%fused_computation.13 | loop fusion | flops 32768 | bytes 16384 | tf_op jit(solution)/shard_map/concatenate | solution.py:69
  (8 shorter events, 0.1 us)
Async XLA Ops:
  0.0 10.2 %collective-permute-start.3 = (bf16[768,128]{1,0:T(8,128)(2,1)}, bf16[768,128]{1,0:T(8,128)(2,1)S(1)}, u32[]{:S(2)}, u32[]{:S(2)}) collective-permute-start(bf16[768,128]{1,0:T(8,128)(2,1)} %param.5), channel_id=1, source_target_pairs={{0,8},{8,0},{16,24},{24,16},{1,9},{9,1},{17,25},{25,17},{2,10},{10... | collective-permute-start | bytes 589832 | tf_op jit(solution)/shard_map/ppermute | solution.py:52
  2.9 10.8 %collective-permute-start.4 = (bf16[768,128]{1,0:T(8,128)(2,1)}, bf16[768,128]{1,0:T(8,128)(2,1)S(1)}, u32[]{:S(2)}, u32[]{:S(2)}) collective-permute-start(bf16[768,128]{1,0:T(8,128)(2,1)} %param.5), channel_id=1, source_target_pairs={{0,16},{8,24},{16,0},{24,8},{1,17},{9,25},{17,1},{25,9},{2,18},{10... | collective-permute-start | bytes 589832 | tf_op jit(solution)/shard_map/ppermute | solution.py:52
  4.5 9.3 %collective-permute-start.5 = (bf16[768,128]{1,0:T(8,128)(2,1)}, bf16[768,128]{1,0:T(8,128)(2,1)S(1)}, u32[]{:S(2)}, u32[]{:S(2)}) collective-permute-start(bf16[768,128]{1,0:T(8,128)(2,1)} %param.5), channel_id=1, source_target_pairs={{0,24},{8,16},{16,8},{24,0},{1,25},{9,17},{17,9},{25,1},{2,26},{10... | collective-permute-start | bytes 589832 | tf_op jit(solution)/shard_map/ppermute | solution.py:52
  6.1 8.7 %collective-permute-start = (bf16[8,1536]{1,0:T(8,128)(2,1)}, bf16[8,1536]{1,0:T(8,128)(2,1)S(1)}, u32[]{:S(2)}, u32[]{:S(2)}) collective-permute-start(bf16[8,1536]{1,0:T(8,128)(2,1)} %get-tuple-element.12), channel_id=1, source_target_pairs={{0,6},{1,7},{2,4},{3,5},{4,2},{5,3},{6,0},{7,1},{8,14},{9,15},{10,... | collective-permute-start | bytes 73736 | tf_op jit(solution)/shard_map/ppermute | solution.py:52
  10.2 4.9 %collective-permute-start.1 = (bf16[8,1536]{1,0:T(8,128)(2,1)}, bf16[8,1536]{1,0:T(8,128)(2,1)S(1)}, u32[]{:S(2)}, u32[]{:S(2)}) collective-permute-start(bf16[8,1536]{1,0:T(8,128)(2,1)} %get-tuple-element.13), channel_id=1, source_target_pairs={{0,4},{1,5},{2,6},{3,7},{4,0},{5,1},{6,2},{7,3},{8,12},{9,13},{10,... | collective-permute-start | bytes 73736 | tf_op jit(solution)/shard_map/ppermute | solution.py:52
  10.2 4.6 %copy-start = (bf16[8,1536]{1,0:T(8,128)(2,1)S(1)}, bf16[8,1536]{1,0:T(8,128)(2,1)}, u32[]{:S(2)}) copy-start(bf16[8,1536]{1,0:T(8,128)(2,1)} %get-tuple-element.11) | copy-start | bytes 73732
  10.2 4.5 %collective-permute-start.2 = (bf16[8,1536]{1,0:T(8,128)(2,1)}, bf16[8,1536]{1,0:T(8,128)(2,1)S(1)}, u32[]{:S(2)}, u32[]{:S(2)}) collective-permute-start(bf16[8,1536]{1,0:T(8,128)(2,1)} %get-tuple-element.14), channel_id=1, source_target_pairs={{0,2},{1,3},{2,0},{3,1},{4,6},{5,7},{6,4},{7,5},{8,10},{9,11},{10,... | collective-permute-start | bytes 73736 | tf_op jit(solution)/shard_map/ppermute | solution.py:52
  14.8 2.4 %collective-permute-start.6 = (bf16[768,512]{1,0:T(8,128)(2,1)S(1)}, bf16[768,512]{1,0:T(8,128)(2,1)S(1)}, u32[]{:S(2)}, u32[]{:S(2)}) collective-permute-start(bf16[768,512]{1,0:T(8,128)(2,1)S(1)} %pad_maximum_fusion), channel_id=1, source_target_pairs={{0,1},{1,0},{2,3},{3,2},{4,5},{5,4},{6,7},{7,6},{8,9},{9,8},{10,11... | collective-permute-start | bytes 2359304 | tf_op jit(solution)/shard_map/ppermute | solution.py:52
  17.6 5.6 %collective-permute-start.7 = (f32[8,512]{1,0:T(8,128)S(1)}, f32[8,512]{1,0:T(8,128)S(1)}, u32[]{:S(2)}, u32[]{:S(2)}) collective-permute-start(f32[8,512]{1,0:T(8,128)S(1)} %get-tuple-element.17), channel_id=1, source_target_pairs={{0,6},{1,7},{2,4},{3,5},{4,2},{5,3},{6,0},{7,1},{8,14},{9,15},{10,... | collective-permute-start | bytes 49160 | tf_op jit(solution)/shard_map/ppermute | solution.py:52
  21.3 4.6 %collective-permute-start.8 = (f32[8,512]{1,0:T(8,128)S(1)}, f32[8,512]{1,0:T(8,128)S(1)}, u32[]{:S(2)}, u32[]{:S(2)}) collective-permute-start(f32[8,512]{1,0:T(8,128)S(1)} %get-tuple-element.19), channel_id=1, source_target_pairs={{0,4},{1,5},{2,6},{3,7},{4,0},{5,1},{6,2},{7,3},{8,12},{9,13},{10,... | collective-permute-start | bytes 49160 | tf_op jit(solution)/shard_map/ppermute | solution.py:52
  21.3 4.6 %collective-permute-start.9 = (f32[8,512]{1,0:T(8,128)S(1)}, f32[8,512]{1,0:T(8,128)S(1)}, u32[]{:S(2)}, u32[]{:S(2)}) collective-permute-start(f32[8,512]{1,0:T(8,128)S(1)} %get-tuple-element.18), channel_id=1, source_target_pairs={{0,2},{1,3},{2,0},{3,1},{4,6},{5,7},{6,4},{7,5},{8,10},{9,11},{10,... | collective-permute-start | bytes 49160 | tf_op jit(solution)/shard_map/ppermute | solution.py:52

commit v2 on v1

v2 whole, which is shorter than its diff:
```python
import functools
import math

import jax
import jax.numpy as jnp
from jax import lax
from jax.experimental import pallas as pl
from jax.experimental.pallas import tpu as pltpu
from jax.sharding import PartitionSpec as P

CORES = 2
VMEM = pl.BlockSpec(memory_space=pltpu.VMEM)
SMEM = pl.BlockSpec(memory_space=pltpu.SMEM)


def local_call(kernel, name, out_shape, in_specs, operands, cost=None):
    arrays = [*operands, *jax.tree.leaves(out_shape)]
    held = sum(math.prod(a.shape) * a.dtype.itemsize for a in arrays)
    return pl.pallas_call(
        kernel,
        out_shape=out_shape,
        in_specs=in_specs,
        out_specs=jax.tree.map(lambda _: VMEM, out_shape),
        name=name,
        cost_estimate=cost,
        compiler_params=pltpu.CompilerParams(vmem_limit_bytes=held + (2 << 20)),
    )(*operands)


def lane_kernel(lane_ref):
    lane_ref[...] = lax.broadcasted_iota(jnp.int32, lane_ref.shape, 1)


def mask_kernel(order, lane_ref, mask_ref, size_ref, amplitude_ref, *out_refs):
    grp = lax.axis_index("grp")
    chip, core = grp // CORES, lax.rem(grp, CORES)
    lane = lane_ref[...]
    tile = lane.shape[1]
    tiles = out_refs[0].shape[1] // tile // CORES
    for out_ref, step in zip(out_refs, order):
        for half in range(CORES):
            first = ((chip ^ step) * CORES + (core ^ half)) * tiles
            for t in range(tiles):
                k = first + t
                live = jnp.where(mask_ref[0, k] == 1, size_ref[k], 0)
                value = amplitude_ref[:, pl.ds(pl.multiple_of(k * tile, tile), tile)]
                place = (half * tiles + t) * tile
                out_ref[:, place : place + tile] = jnp.where(lane < live, value, jnp.zeros_like(value))


def dot_kernel(members, blocks, *refs):
    live_refs, own_refs, other_refs = refs[:members], refs[members : members + blocks], refs[members + blocks : -1]
    out_ref = refs[-1]
    blk = lax.axis_index("blk")
    depth, cols = own_refs[0].shape
    live = jnp.concatenate([ref[...] for ref in live_refs], axis=0)
    for step, (own_ref, other_ref) in enumerate(zip(own_refs, other_refs)):
        total = jnp.dot(live[:, :depth], own_ref[...], preferred_element_type=jnp.float32)
        total += jnp.dot(live[:, depth:], other_ref[...], preferred_element_type=jnp.float32)
        out_ref[:, pl.ds(pl.multiple_of((blk ^ step) * cols, cols), cols)] = total


def after(received, places, value):
    *arrived, value = lax.optimization_barrier((*[received[k] for k in places], value))
    for k, array in zip(places, arrived):
        received[k] = array
    return value


def body(blk_size, grp_size, amplitudes, integrals, tile_mask, tile_size):
    rows, width = amplitudes.shape
    depth, cols = integrals.shape
    chips = grp_size // CORES
    chip = lax.axis_index("grp") // CORES

    def swap(array, axis, size, step):
        return lax.ppermute(array, axis, [(k, k ^ step) for k in range(size)])

    def shift(array, step):
        pairs = [(k, (k // CORES + step) % chips * CORES + k % CORES) for k in range(grp_size)]
        return lax.ppermute(array, "grp", pairs)

    own = [integrals] + [swap(integrals, "blk", blk_size, step) for step in range(1, blk_size)]

    lane = local_call(
        lane_kernel,
        "lane",
        jax.ShapeDtypeStruct((rows, width // tile_size.shape[0]), jnp.int32),
        [],
        [],
        pl.CostEstimate(flops=10**9, bytes_accessed=0, transcendentals=0),
    )
    order = (0, *range(chips - 1, 0, -1))
    block = jax.ShapeDtypeStruct((rows, CORES * depth), amplitudes.dtype)
    blocks = local_call(
        functools.partial(mask_kernel, order),
        "live_blocks",
        [block] * chips,
        [VMEM, SMEM, SMEM, VMEM],
        [lane, tile_mask, tile_size, amplitudes],
    )
    blocks = list(blocks)
    if blk_size > 1:
        blocks[-1], own[1] = lax.optimization_barrier((blocks[-1], own[1]))
    received = [blocks[0]] + [swap(b, "grp", grp_size, CORES * step) for b, step in zip(blocks[1:], order[1:])]

    other = []
    for step in range(blk_size):
        places = range(1, chips) if step > 1 else range(1, min(2, chips))
        own[step] = after(received, places, own[step])
        other.append(swap(own[step], "grp", grp_size, 1))

    partial = local_call(
        functools.partial(dot_kernel, chips, blk_size),
        "dots",
        jax.ShapeDtypeStruct((chips * rows, blk_size * cols), jnp.float32),
        [VMEM] * (chips + 2 * blk_size),
        [*received, *own, *other],
    )
    ladder = partial[:rows]
    for step in range(1, chips):
        place = chips - (chip ^ lax.rem(chip + step, chips))
        ladder += shift(lax.dynamic_slice_in_dim(partial, place * rows, rows), step)
    return ladder.astype(jnp.bfloat16)


def solution(mesh):
    return jax.shard_map(
        functools.partial(body, mesh.shape["blk"], mesh.shape["grp"]),
        mesh=mesh,
        in_specs=(P(("blk", "grp"), None), P("grp", "blk"), P(("blk", "grp"), None), P()),
        out_specs=P(("blk", "grp"), None),
        check_vma=False,
    )
```

time: 26.7 us -> 24.6 us (0.921)
  starting transfers between devices: 13.9 us -> 16 us
  waiting for transfers between devices: 8.78 us -> 6.76 us
  other arithmetic: 1.64 us -> 0.61 us
  Pallas kernels: 1.68 us -> 1.02 us
  matrix products: 0.47 us -> 0 us
    ppermute x10 -> x13, starting transfers between devices: 13.9 us -> 16 us  [the longest x10 11 us: swap(): return lax.ppermute(array, axis, [(k, k ^ step) for k in range(size)])]
    ppermute x10 -> x13, waiting for transfers between devices: 8.78 us -> 6.76 us  [the longest x10 4.38 us: swap(): return lax.ppermute(array, axis, [(k, k ^ step) for k in range(size)])]
    concatenate x2 -> x0, other arithmetic: 1.62 us -> none  [the longest x1 1.01 us: body(): jnp.concatenate([integrals] + [between(integrals, 'blk', blk_size, step)...]
    pallas_call x1 -> x3, Pallas kernels: 1.68 us -> 1.02 us  [local_call(): pl.pallas_call(kernel, out_shape=out_shape, in_specs=in_specs, out_specs=...]
    convert_element_type x1, other arithmetic: 0.01 us -> 0.61 us  [body(): return ladder.astype(jnp.bfloat16)]
    dot_general x2 -> x0, matrix products: 0.47 us -> none  [the longest x1 0.24 us: body(): partial = jnp.dot(live[:, :depth], own, preferred_element_type=jnp.float32)]
  transfers between devices with their start and end apart: 10 -> 13, of which waited for: 5 -> 8; matrix products, arithmetic and copies ran while one was open for 4% -> 0% of each run, Pallas kernels for 6% -> 3%
where the time goes in v2:
time: 24.6 us; the launch traced here: 24.5 us
  starting transfers between devices  16 us (65%)
  waiting for transfers between devices  6.76 us (27%)
  Pallas kernels  1.02 us (4%)
  other arithmetic  0.61 us (2%)
    ppermute x10, starting transfers between devices, swap(): return lax.ppermute(array, axis, [(k, k ^ step) for k in range(size)])  11 us
    ppermute x3, starting transfers between devices, shift(): return lax.ppermute(array, 'grp', pairs)  4.96 us
    ppermute x10, waiting for transfers between devices, swap(): return lax.ppermute(array, axis, [(k, k ^ step) for k in range(size)])  4.38 us
    ppermute x3, waiting for transfers between devices, shift(): return lax.ppermute(array, 'grp', pairs)  2.39 us
    pallas_call x3, Pallas kernels, local_call(): pl.pallas_call(kernel, out_shape=out_shape, in_specs=in_specs, out_specs=...  1.02 us
    convert_element_type x1, other arithmetic, body(): return ladder.astype(jnp.bfloat16)  0.61 us
  transfers between devices with their start and end apart: 13, of which 8 were waited for; matrix products, arithmetic and copies ran while one was open for 0% of the time, Pallas kernels for 3%

profile of v2, /device:TPU:0, one launch (start us, length us, event | category | flops | bytes accessed | tf_op | source)
XLA Modules:
  0.0 24.5 jit_solution(10420100241947213876)
XLA Ops:
  0.0 0.0 copy-start
  0.0 0.0 copy-start.1
  0.0 0.0 copy-start.2
  0.0 0.0 copy-start.3
  0.0 3.0 %collective-permute-start.1 = (bf16[768,128]{1,0:T(8,128)(2,1)}, bf16[768,128]{1,0:T(8,128)(2,1)S(1)}, u32[]{:S(2)}, u32[]{:S(2)}) collective-permute-start(bf16[768,128]{1,0:T(8,128)(2,1)} %refs_4_), channel_id=1, source_target_pairs={{0,8},{8,0},{16,24},{24,16},{1,9},{9,1},{17,25},{25,17},{2,10},{10... | collective-permute-start | bytes 589832 | tf_op jit(solution)/shard_map/ppermute | solution.py:77
  3.0 1.5 %collective-permute-start.4 = (bf16[768,128]{1,0:T(8,128)(2,1)}, bf16[768,128]{1,0:T(8,128)(2,1)S(1)}, u32[]{:S(2)}, u32[]{:S(2)}) collective-permute-start(bf16[768,128]{1,0:T(8,128)(2,1)} %refs_4_), channel_id=1, source_target_pairs={{0,16},{8,24},{16,0},{24,8},{1,17},{9,25},{17,1},{25,9},{2,18},{10... | collective-permute-start | bytes 589832 | tf_op jit(solution)/shard_map/ppermute | solution.py:77
  4.5 0.0 collective-permute-start.5
  4.6 0.0 copy-done.1
  4.6 0.0 copy-done.2
  4.6 0.0 copy-done.3
  4.6 0.7 %live_blocks.1 = (bf16[8,1536]{1,0:T(8,128)(2,1)S(1)}, bf16[8,1536]{1,0:T(8,128)(2,1)S(1)}, bf16[8,1536]{1,0:T(8,128)(2,1)S(1)}, bf16[8,1536]{1,0:T(8,128)(2,1)S(1)}) custom-call(s32[8,128]{1,0:T(8,128)S(1)} %lane.1.lane_ref, s32[1,48]{1,0:T(1,128)S(1)} %copy-done.2, s32[48]{0:T(128)S(1)} %copy-done.3, bf16[8,6144]{1,0:T(8,128)(2,1)S(1)} %copy-done.1), custom_call_target="tpu_custom_call" | custom-call | tf_op jit(solution)/shard_map/live_blocks/pallas_call | solution.py:19
  5.3 4.1 %collective-permute-start = (bf16[8,1536]{1,0:T(8,128)(2,1)S(1)}, bf16[8,1536]{1,0:T(8,128)(2,1)S(1)}, u32[]{:S(2)}, u32[]{:S(2)}) collective-permute-start(bf16[8,1536]{1,0:T(8,128)(2,1)S(1)} %get-tuple-element.24), channel_id=1, source_target_pairs={{0,6},{1,7},{2,4},{3,5},{4,2},{5,3},{6,0},{7,1},{8,14},{9,15},{10,... | collective-permute-start | bytes 73736 | tf_op jit(solution)/shard_map/ppermute | solution.py:77
  9.4 0.0 collective-permute-start.2
  9.4 0.0 collective-permute-done.1.refs_5_
  9.4 1.7 %collective-permute-start.3 = (bf16[8,1536]{1,0:T(8,128)(2,1)S(1)}, bf16[8,1536]{1,0:T(8,128)(2,1)S(1)}, u32[]{:S(2)}, u32[]{:S(2)}) collective-permute-start(bf16[8,1536]{1,0:T(8,128)(2,1)S(1)} %get-tuple-element.30), channel_id=1, source_target_pairs={{0,2},{1,3},{2,0},{3,1},{4,6},{5,7},{6,4},{7,5},{8,10},{9,11},{10,... | collective-permute-start | bytes 73736 | tf_op jit(solution)/shard_map/ppermute | solution.py:77
  11.1 0.1 collective-permute-done.refs_1_
  11.2 0.0 copy-done
  11.2 0.0 collective-permute-start.6
  11.2 2.9 %collective-permute-done.2.refs_2_ = bf16[8,1536]{1,0:T(8,128)(2,1)S(1)} collective-permute-done((bf16[8,1536]{1,0:T(8,128)(2,1)S(1)}, bf16[8,1536]{1,0:T(8,128)(2,1)S(1)}, u32[]{:S(2)}, u32[]{:S(2)}) %collective-permute-start.2) | collective-permute-done | bytes 24608 | tf_op jit(solution)/shard_map/ppermute | solution.py:77
  14.1 0.0 collective-permute-start.7
  14.1 0.0 collective-permute-done.4.refs_6_
  14.1 0.0 collective-permute-done.3.refs_3_
  14.1 0.0 collective-permute-done.5.refs_7_
  14.1 0.6 %collective-permute-start.9 = (bf16[768,128]{1,0:T(8,128)(2,1)S(1)}, bf16[768,128]{1,0:T(8,128)(2,1)S(1)}, u32[]{:S(2)}, u32[]{:S(2)}) collective-permute-start(bf16[768,128]{1,0:T(8,128)(2,1)S(1)} %collective-permute-done.5.refs_7_), channel_id=1, source_target_pairs={{0,1},{1,0},{2,3},{3,2},{4,5},{5,4},{6,7},{7,6},{8,9},{9,8},{10,11... | collective-permute-start | bytes 589832 | tf_op jit(solution)/shard_map/ppermute | solution.py:77
  14.7 0.1 collective-permute-start.8
  14.8 0.0 collective-permute-done.6.refs_8_
  14.8 0.8 %collective-permute-done.7.refs_9_ = bf16[768,128]{1,0:T(8,128)(2,1)S(1)} collective-permute-done((bf16[768,128]{1,0:T(8,128)(2,1)S(1)}, bf16[768,128]{1,0:T(8,128)(2,1)S(1)}, u32[]{:S(2)}, u32[]{:S(2)}) %collective-permute-start.7) | collective-permute-done | bytes 196640 | tf_op jit(solution)/shard_map/ppermute | solution.py:77
  15.6 0.3 %collective-permute-done.9.refs_11_ = bf16[768,128]{1,0:T(8,128)(2,1)S(1)} collective-permute-done((bf16[768,128]{1,0:T(8,128)(2,1)S(1)}, bf16[768,128]{1,0:T(8,128)(2,1)S(1)}, u32[]{:S(2)}, u32[]{:S(2)}) %collective-permute-start.9) | collective-permute-done | bytes 196640 | tf_op jit(solution)/shard_map/ppermute | solution.py:77
  15.8 0.3 %collective-permute-done.8.refs_10_ = bf16[768,128]{1,0:T(8,128)(2,1)S(1)} collective-permute-done((bf16[768,128]{1,0:T(8,128)(2,1)S(1)}, bf16[768,128]{1,0:T(8,128)(2,1)S(1)}, u32[]{:S(2)}, u32[]{:S(2)}) %collective-permute-start.8) | collective-permute-done | bytes 196640 | tf_op jit(solution)/shard_map/ppermute | solution.py:77
  16.1 0.3 %dots.1 = f32[32,512]{1,0:T(8,128)S(1)} custom-call(bf16[8,1536]{1,0:T(8,128)(2,1)S(1)} %get-tuple-element.23.refs_0_, bf16[8,1536]{1,0:T(8,128)(2,1)S(1)} %collective-permute-done.refs_1_, bf16[8,1536]{1,0:T(8,128)(2,1)S(1)} %collective-permute-done.2.refs_2_, bf16[8,1536]{1,0:T(8,128)(2,1)S(1)} %collective-permute-done.3.refs_3_, ...), custom_call_target="tpu_custom_call" | custom-call | tf_op jit(solution)/shard_map/dots/pallas_call | solution.py:19
  16.5 1.0 %collective-permute-start.10 = (f32[8,512]{1,0:T(8,128)S(1)}, f32[8,512]{1,0:T(8,128)S(1)}, u32[]{:S(2)}, u32[]{:S(2)}) collective-permute-start(f32[8,512]{1,0:T(8,128)S(1)} %get-tuple-element.41), channel_id=1, source_target_pairs={{0,2},{1,3},{2,4},{3,5},{4,6},{5,7},{6,0},{7,1},{8,10},{9,11},{10,... | collective-permute-start | bytes 49160 | tf_op jit(solution)/shard_map/ppermute | solution.py:81
  17.5 2.6 %collective-permute-start.11 = (f32[8,512]{1,0:T(8,128)S(1)}, f32[8,512]{1,0:T(8,128)S(1)}, u32[]{:S(2)}, u32[]{:S(2)}) collective-permute-start(f32[8,512]{1,0:T(8,128)S(1)} %get-tuple-element.43), channel_id=1, source_target_pairs={{0,4},{1,5},{2,6},{3,7},{4,0},{5,1},{6,2},{7,3},{8,12},{9,13},{10,... | collective-permute-start | bytes 49160 | tf_op jit(solution)/shard_map/ppermute | solution.py:81
  20.1 1.3 %collective-permute-start.12 = (f32[8,512]{1,0:T(8,128)S(1)}, f32[8,512]{1,0:T(8,128)S(1)}, u32[]{:S(2)}, u32[]{:S(2)}) collective-permute-start(f32[8,512]{1,0:T(8,128)S(1)} %get-tuple-element.42), channel_id=1, source_target_pairs={{0,6},{1,7},{2,0},{3,1},{4,2},{5,3},{6,4},{7,5},{8,14},{9,15},{10,... | collective-permute-start | bytes 49160 | tf_op jit(solution)/shard_map/ppermute | solution.py:81
  21.5 0.8 %collective-permute-done.10 = f32[8,512]{1,0:T(8,128)S(1)} collective-permute-done((f32[8,512]{1,0:T(8,128)S(1)}, f32[8,512]{1,0:T(8,128)S(1)}, u32[]{:S(2)}, u32[]{:S(2)}) %collective-permute-start.10) | collective-permute-done | bytes 16416 | tf_op jit(solution)/shard_map/ppermute | solution.py:81
  22.2 0.2 collective-permute-done.11
  22.5 1.4 %collective-permute-done.12 = f32[8,512]{1,0:T(8,128)S(1)} collective-permute-done((f32[8,512]{1,0:T(8,128)S(1)}, f32[8,512]{1,0:T(8,128)S(1)}, u32[]{:S(2)}, u32[]{:S(2)}) %collective-permute-start.12) | collective-permute-done | bytes 16416 | tf_op jit(solution)/shard_map/ppermute | solution.py:81
  23.9 0.6 %fusion.2 = bf16[8,512]{1,0:T(8,128)(2,1)} fusion(f32[8,512]{1,0:T(8,128)S(1)} %collective-permute-done.12, f32[8,512]{1,0:T(8,128)S(1)} %collective-permute-done.11, f32[8,512]{1,0:T(8,128)S(1)} %collective-permute-done.10, f32[32,512]{1,0:T(8,128)S(1)} %dots.1), kind=kLoop, calls=%fused_computation.3 | loop fusion | flops 16384 | bytes 73728 | tf_op jit(solution)/shard_map/convert_element_type | solution.py:124
  (2 shorter events, 0.0 us)
Async XLA Ops:
  0.0 11.2 %copy-start = (bf16[768,128]{1,0:T(8,128)(2,1)S(1)}, bf16[768,128]{1,0:T(8,128)(2,1)}, u32[]{:S(2)}) copy-start(bf16[768,128]{1,0:T(8,128)(2,1)} %refs_4_) | copy-start | bytes 589828
  0.0 4.6 %copy-start.1 = (bf16[8,6144]{1,0:T(8,128)(2,1)S(1)}, bf16[8,6144]{1,0:T(8,128)(2,1)}, u32[]{:S(2)}) copy-start(bf16[8,6144]{1,0:T(8,128)(2,1)} %amplitude_ref.1) | copy-start | bytes 294916
  0.0 4.6 %copy-start.2 = (s32[1,48]{1,0:T(1,128)S(1)}, s32[1,48]{1,0:T(1,128)}, u32[]{:S(2)}) copy-start(s32[1,48]{1,0:T(1,128)} %mask_ref.1) | copy-start | bytes 580
  0.0 4.6 %copy-start.3 = (s32[48]{0:T(128)S(1)}, s32[48]{0:T(128)}, u32[]{:S(2)}) copy-start(s32[48]{0:T(128)} %size_ref.1) | copy-start | bytes 580
  0.0 9.4 %collective-permute-start.1 = (bf16[768,128]{1,0:T(8,128)(2,1)}, bf16[768,128]{1,0:T(8,128)(2,1)S(1)}, u32[]{:S(2)}, u32[]{:S(2)}) collective-permute-start(bf16[768,128]{1,0:T(8,128)(2,1)} %refs_4_), channel_id=1, source_target_pairs={{0,8},{8,0},{16,24},{24,16},{1,9},{9,1},{17,25},{25,17},{2,10},{10... | collective-permute-start | bytes 589832 | tf_op jit(solution)/shard_map/ppermute | solution.py:77
  3.0 11.1 %collective-permute-start.4 = (bf16[768,128]{1,0:T(8,128)(2,1)}, bf16[768,128]{1,0:T(8,128)(2,1)S(1)}, u32[]{:S(2)}, u32[]{:S(2)}) collective-permute-start(bf16[768,128]{1,0:T(8,128)(2,1)} %refs_4_), channel_id=1, source_target_pairs={{0,16},{8,24},{16,0},{24,8},{1,17},{9,25},{17,1},{25,9},{2,18},{10... | collective-permute-start | bytes 589832 | tf_op jit(solution)/shard_map/ppermute | solution.py:77
  4.5 9.6 %collective-permute-start.5 = (bf16[768,128]{1,0:T(8,128)(2,1)}, bf16[768,128]{1,0:T(8,128)(2,1)S(1)}, u32[]{:S(2)}, u32[]{:S(2)}) collective-permute-start(bf16[768,128]{1,0:T(8,128)(2,1)} %refs_4_), channel_id=1, source_target_pairs={{0,24},{8,16},{16,8},{24,0},{1,25},{9,17},{17,9},{25,1},{2,26},{10... | collective-permute-start | bytes 589832 | tf_op jit(solution)/shard_map/ppermute | solution.py:77
  5.3 6.0 %collective-permute-start = (bf16[8,1536]{1,0:T(8,128)(2,1)S(1)}, bf16[8,1536]{1,0:T(8,128)(2,1)S(1)}, u32[]{:S(2)}, u32[]{:S(2)}) collective-permute-start(bf16[8,1536]{1,0:T(8,128)(2,1)S(1)} %get-tuple-element.24), channel_id=1, source_target_pairs={{0,6},{1,7},{2,4},{3,5},{4,2},{5,3},{6,0},{7,1},{8,14},{9,15},{10,... | collective-permute-start | bytes 73736 | tf_op jit(solution)/shard_map/ppermute | solution.py:77
  9.4 4.7 %collective-permute-start.2 = (bf16[8,1536]{1,0:T(8,128)(2,1)S(1)}, bf16[8,1536]{1,0:T(8,128)(2,1)S(1)}, u32[]{:S(2)}, u32[]{:S(2)}) collective-permute-start(bf16[8,1536]{1,0:T(8,128)(2,1)S(1)} %get-tuple-element.29), channel_id=1, source_target_pairs={{0,4},{1,5},{2,6},{3,7},{4,0},{5,1},{6,2},{7,3},{8,12},{9,13},{10,... | collective-permute-start | bytes 73736 | tf_op jit(solution)/shard_map/ppermute | solution.py:77
  9.4 4.7 %collective-permute-start.3 = (bf16[8,1536]{1,0:T(8,128)(2,1)S(1)}, bf16[8,1536]{1,0:T(8,128)(2,1)S(1)}, u32[]{:S(2)}, u32[]{:S(2)}) collective-permute-start(bf16[8,1536]{1,0:T(8,128)(2,1)S(1)} %get-tuple-element.30), channel_id=1, source_target_pairs={{0,2},{1,3},{2,0},{3,1},{4,6},{5,7},{6,4},{7,5},{8,10},{9,11},{10,... | collective-permute-start | bytes 73736 | tf_op jit(solution)/shard_map/ppermute | solution.py:77
  11.2 3.6 %collective-permute-start.6 = (bf16[768,128]{1,0:T(8,128)(2,1)S(1)}, bf16[768,128]{1,0:T(8,128)(2,1)S(1)}, u32[]{:S(2)}, u32[]{:S(2)}) collective-permute-start(bf16[768,128]{1,0:T(8,128)(2,1)S(1)} %copy-done), channel_id=1, source_target_pairs={{0,1},{1,0},{2,3},{3,2},{4,5},{5,4},{6,7},{7,6},{8,9},{9,8},{10,11... | collective-permute-start | bytes 589832 | tf_op jit(solution)/shard_map/ppermute | solution.py:77
  14.1 1.4 %collective-permute-start.7 = (bf16[768,128]{1,0:T(8,128)(2,1)S(1)}, bf16[768,128]{1,0:T(8,128)(2,1)S(1)}, u32[]{:S(2)}, u32[]{:S(2)}) collective-permute-start(bf16[768,128]{1,0:T(8,128)(2,1)S(1)} %collective-permute-done.1.refs_5_), channel_id=1, source_target_pairs={{0,1},{1,0},{2,3},{3,2},{4,5},{5,4},{6,7},{7,6},{8,9},{9,8},{10,11... | collective-permute-start | bytes 589832 | tf_op jit(solution)/shard_map/ppermute | solution.py:77
  14.1 1.7 %collective-permute-start.9 = (bf16[768,128]{1,0:T(8,128)(2,1)S(1)}, bf16[768,128]{1,0:T(8,128)(2,1)S(1)}, u32[]{:S(2)}, u32[]{:S(2)}) collective-permute-start(bf16[768,128]{1,0:T(8,128)(2,1)S(1)} %collective-permute-done.5.refs_7_), channel_id=1, source_target_pairs={{0,1},{1,0},{2,3},{3,2},{4,5},{5,4},{6,7},{7,6},{8,9},{9,8},{10,11... | collective-permute-start | bytes 589832 | tf_op jit(solution)/shard_map/ppermute | solution.py:77
  14.7 1.4 %collective-permute-start.8 = (bf16[768,128]{1,0:T(8,128)(2,1)S(1)}, bf16[768,128]{1,0:T(8,128)(2,1)S(1)}, u32[]{:S(2)}, u32[]{:S(2)}) collective-permute-start(bf16[768,128]{1,0:T(8,128)(2,1)S(1)} %collective-permute-done.4.refs_6_), channel_id=1, source_target_pairs={{0,1},{1,0},{2,3},{3,2},{4,5},{5,4},{6,7},{7,6},{8,9},{9,8},{10,11... | collective-permute-start | bytes 589832 | tf_op jit(solution)/shard_map/ppermute | solution.py:77
  16.5 5.7 %collective-permute-start.10 = (f32[8,512]{1,0:T(8,128)S(1)}, f32[8,512]{1,0:T(8,128)S(1)}, u32[]{:S(2)}, u32[]{:S(2)}) collective-permute-start(f32[8,512]{1,0:T(8,128)S(1)} %get-tuple-element.41), channel_id=1, source_target_pairs={{0,2},{1,3},{2,4},{3,5},{4,6},{5,7},{6,0},{7,1},{8,10},{9,11},{10,... | collective-permute-start | bytes 49160 | tf_op jit(solution)/shard_map/ppermute | solution.py:81
  17.5 4.9 %collective-permute-start.11 = (f32[8,512]{1,0:T(8,128)S(1)}, f32[8,512]{1,0:T(8,128)S(1)}, u32[]{:S(2)}, u32[]{:S(2)}) collective-permute-start(f32[8,512]{1,0:T(8,128)S(1)} %get-tuple-element.43), channel_id=1, source_target_pairs={{0,4},{1,5},{2,6},{3,7},{4,0},{5,1},{6,2},{7,3},{8,12},{9,13},{10,... | collective-permute-start | bytes 49160 | tf_op jit(solution)/shard_map/ppermute | solution.py:81
  20.1 3.7 %collective-permute-start.12 = (f32[8,512]{1,0:T(8,128)S(1)}, f32[8,512]{1,0:T(8,128)S(1)}, u32[]{:S(2)}, u32[]{:S(2)}) collective-permute-start(f32[8,512]{1,0:T(8,128)S(1)} %get-tuple-element.42), channel_id=1, source_target_pairs={{0,6},{1,7},{2,0},{3,1},{4,2},{5,3},{6,4},{7,5},{8,14},{9,15},{10,... | collective-permute-start | bytes 49160 | tf_op jit(solution)/shard_map/ppermute | solution.py:81

commit v3 on v2

--- a/solution.py
+++ b/solution.py
@@ -80,8 +80,6 @@
         pairs = [(k, (k // CORES + step) % chips * CORES + k % CORES) for k in range(grp_size)]
         return lax.ppermute(array, "grp", pairs)
 
-    own = [integrals] + [swap(integrals, "blk", blk_size, step) for step in range(1, blk_size)]
-
     lane = local_call(
         lane_kernel,
         "lane",
@@ -90,6 +88,10 @@
         [],
         pl.CostEstimate(flops=10**9, bytes_accessed=0, transcendentals=0),
     )
+
+    lane, later = lax.optimization_barrier((lane, integrals))
+    own = [integrals] + [swap(integrals if step == 1 else later, "blk", blk_size, step) for step in range(1, blk_size)]
+
     order = (0, *range(chips - 1, 0, -1))
     block = jax.ShapeDtypeStruct((rows, CORES * depth), amplitudes.dtype)
     blocks = local_call(

time: 24.6 us -> 24.4 us (level)
  starting transfers between devices: 16 us -> 15.7 us
    ppermute x10, waiting for transfers between devices: 4.38 us -> 4.68 us  [swap(): return lax.ppermute(array, axis, [(k, k ^ step) for k in range(size)])]
    ppermute x3, waiting for transfers between devices: 2.39 us -> 2.13 us  [shift(): return lax.ppermute(array, 'grp', pairs)]
    ppermute x3, starting transfers between devices: 4.96 us -> 4.7 us  [shift(): return lax.ppermute(array, 'grp', pairs)]
  transfers between devices with their start and end apart: 13 -> 13, of which waited for: 8 -> 7; matrix products, arithmetic and copies ran while one was open for 0% -> 0% of each run, Pallas kernels for 3% -> 3%
where the time goes in v3:
time: 24.4 us; the launch traced here: 24.3 us
  starting transfers between devices  15.7 us (64%)
  waiting for transfers between devices  6.81 us (28%)
  Pallas kernels  1.02 us (4%)
  other arithmetic  0.61 us (2%)
    ppermute x10, starting transfers between devices, swap(): return lax.ppermute(array, axis, [(k, k ^ step) for k in range(size)])  11 us
    ppermute x3, starting transfers between devices, shift(): return lax.ppermute(array, 'grp', pairs)  4.7 us
    ppermute x10, waiting for transfers between devices, swap(): return lax.ppermute(array, axis, [(k, k ^ step) for k in range(size)])  4.68 us
    ppermute x3, waiting for transfers between devices, shift(): return lax.ppermute(array, 'grp', pairs)  2.13 us
    pallas_call x3, Pallas kernels, local_call(): pl.pallas_call(kernel, out_shape=out_shape, in_specs=in_specs, out_specs=...  1.02 us
    convert_element_type x1, other arithmetic, body(): return ladder.astype(jnp.bfloat16)  0.61 us
  transfers between devices with their start and end apart: 13, of which 7 were waited for; matrix products, arithmetic and copies ran while one was open for 0% of the time, Pallas kernels for 3%

profile of v3, /device:TPU:0, one launch (start us, length us, event | category | flops | bytes accessed | tf_op | source)
XLA Modules:
  0.0 24.3 jit_solution(3843252833458929377)
XLA Ops:
  0.0 0.0 copy-start
  0.0 0.0 copy-start.1
  0.0 0.0 copy-start.2
  0.0 0.0 copy-start.3
  0.0 3.0 %collective-permute-start.1 = (bf16[768,128]{1,0:T(8,128)(2,1)}, bf16[768,128]{1,0:T(8,128)(2,1)S(1)}, u32[]{:S(2)}, u32[]{:S(2)}) collective-permute-start(bf16[768,128]{1,0:T(8,128)(2,1)} %refs_4_), channel_id=1, source_target_pairs={{0,8},{8,0},{16,24},{24,16},{1,9},{9,1},{17,25},{25,17},{2,10},{10... | collective-permute-start | bytes 589832 | tf_op jit(solution)/shard_map/ppermute | solution.py:77
  3.0 0.0 copy-done
  3.0 1.5 %collective-permute-start.4 = (bf16[768,128]{1,0:T(8,128)(2,1)S(1)}, bf16[768,128]{1,0:T(8,128)(2,1)S(1)}, u32[]{:S(2)}, u32[]{:S(2)}) collective-permute-start(bf16[768,128]{1,0:T(8,128)(2,1)S(1)} %copy-done), channel_id=1, source_target_pairs={{0,16},{8,24},{16,0},{24,8},{1,17},{9,25},{17,1},{25,9},{2,18},{10... | collective-permute-start | bytes 589832 | tf_op jit(solution)/shard_map/ppermute | solution.py:77
  4.5 0.8 %collective-permute-start.5 = (bf16[768,128]{1,0:T(8,128)(2,1)S(1)}, bf16[768,128]{1,0:T(8,128)(2,1)S(1)}, u32[]{:S(2)}, u32[]{:S(2)}) collective-permute-start(bf16[768,128]{1,0:T(8,128)(2,1)S(1)} %copy-done), channel_id=1, source_target_pairs={{0,24},{8,16},{16,8},{24,0},{1,25},{9,17},{17,9},{25,1},{2,26},{10... | collective-permute-start | bytes 589832 | tf_op jit(solution)/shard_map/ppermute | solution.py:77
  5.3 0.0 copy-done.1
  5.3 0.0 copy-done.2
  5.3 0.0 copy-done.3
  5.3 0.7 %live_blocks.1 = (bf16[8,1536]{1,0:T(8,128)(2,1)S(1)}, bf16[8,1536]{1,0:T(8,128)(2,1)S(1)}, bf16[8,1536]{1,0:T(8,128)(2,1)S(1)}, bf16[8,1536]{1,0:T(8,128)(2,1)S(1)}) custom-call(s32[8,128]{1,0:T(8,128)S(1)} %lane.1.lane_ref, s32[1,48]{1,0:T(1,128)S(1)} %copy-done.2, s32[48]{0:T(128)S(1)} %copy-done.3, bf16[8,6144]{1,0:T(8,128)(2,1)S(1)} %copy-done.1), custom_call_target="tpu_custom_call" | custom-call | tf_op jit(solution)/shard_map/live_blocks/pallas_call | solution.py:19
  6.0 3.7 %collective-permute-start = (bf16[8,1536]{1,0:T(8,128)(2,1)S(1)}, bf16[8,1536]{1,0:T(8,128)(2,1)S(1)}, u32[]{:S(2)}, u32[]{:S(2)}) collective-permute-start(bf16[8,1536]{1,0:T(8,128)(2,1)S(1)} %get-tuple-element.27), channel_id=1, source_target_pairs={{0,6},{1,7},{2,4},{3,5},{4,2},{5,3},{6,0},{7,1},{8,14},{9,15},{10,... | collective-permute-start | bytes 73736 | tf_op jit(solution)/shard_map/ppermute | solution.py:77
  9.7 0.0 collective-permute-start.2
  9.7 0.0 collective-permute-done.1.refs_5_
  9.7 1.4 %collective-permute-start.3 = (bf16[8,1536]{1,0:T(8,128)(2,1)S(1)}, bf16[8,1536]{1,0:T(8,128)(2,1)S(1)}, u32[]{:S(2)}, u32[]{:S(2)}) collective-permute-start(bf16[8,1536]{1,0:T(8,128)(2,1)S(1)} %get-tuple-element.33), channel_id=1, source_target_pairs={{0,2},{1,3},{2,0},{3,1},{4,6},{5,7},{6,4},{7,5},{8,10},{9,11},{10,... | collective-permute-start | bytes 73736 | tf_op jit(solution)/shard_map/ppermute | solution.py:77
  11.1 0.7 %collective-permute-done.refs_1_ = bf16[8,1536]{1,0:T(8,128)(2,1)S(1)} collective-permute-done((bf16[8,1536]{1,0:T(8,128)(2,1)S(1)}, bf16[8,1536]{1,0:T(8,128)(2,1)S(1)}, u32[]{:S(2)}, u32[]{:S(2)}) %collective-permute-start) | collective-permute-done | bytes 24608 | tf_op jit(solution)/shard_map/ppermute | solution.py:77
  11.8 0.0 collective-permute-start.6
  11.8 2.6 %collective-permute-done.2.refs_2_ = bf16[8,1536]{1,0:T(8,128)(2,1)S(1)} collective-permute-done((bf16[8,1536]{1,0:T(8,128)(2,1)S(1)}, bf16[8,1536]{1,0:T(8,128)(2,1)S(1)}, u32[]{:S(2)}, u32[]{:S(2)}) %collective-permute-start.2) | collective-permute-done | bytes 24608 | tf_op jit(solution)/shard_map/ppermute | solution.py:77
  14.4 0.0 collective-permute-start.7
  14.4 0.0 collective-permute-done.4.refs_6_
  14.4 0.0 collective-permute-done.3.refs_3_
  14.4 0.0 collective-permute-done.5.refs_7_
  14.4 0.6 %collective-permute-start.9 = (bf16[768,128]{1,0:T(8,128)(2,1)S(1)}, bf16[768,128]{1,0:T(8,128)(2,1)S(1)}, u32[]{:S(2)}, u32[]{:S(2)}) collective-permute-start(bf16[768,128]{1,0:T(8,128)(2,1)S(1)} %collective-permute-done.5.refs_7_), channel_id=1, source_target_pairs={{0,1},{1,0},{2,3},{3,2},{4,5},{5,4},{6,7},{7,6},{8,9},{9,8},{10,11... | collective-permute-start | bytes 589832 | tf_op jit(solution)/shard_map/ppermute | solution.py:77
  15.0 0.1 collective-permute-start.8
  15.1 0.0 collective-permute-done.6.refs_8_
  15.1 0.8 %collective-permute-done.7.refs_9_ = bf16[768,128]{1,0:T(8,128)(2,1)S(1)} collective-permute-done((bf16[768,128]{1,0:T(8,128)(2,1)S(1)}, bf16[768,128]{1,0:T(8,128)(2,1)S(1)}, u32[]{:S(2)}, u32[]{:S(2)}) %collective-permute-start.7) | collective-permute-done | bytes 196640 | tf_op jit(solution)/shard_map/ppermute | solution.py:77
  15.9 0.3 %collective-permute-done.9.refs_11_ = bf16[768,128]{1,0:T(8,128)(2,1)S(1)} collective-permute-done((bf16[768,128]{1,0:T(8,128)(2,1)S(1)}, bf16[768,128]{1,0:T(8,128)(2,1)S(1)}, u32[]{:S(2)}, u32[]{:S(2)}) %collective-permute-start.9) | collective-permute-done | bytes 196640 | tf_op jit(solution)/shard_map/ppermute | solution.py:77
  16.1 0.3 %collective-permute-done.8.refs_10_ = bf16[768,128]{1,0:T(8,128)(2,1)S(1)} collective-permute-done((bf16[768,128]{1,0:T(8,128)(2,1)S(1)}, bf16[768,128]{1,0:T(8,128)(2,1)S(1)}, u32[]{:S(2)}, u32[]{:S(2)}) %collective-permute-start.8) | collective-permute-done | bytes 196640 | tf_op jit(solution)/shard_map/ppermute | solution.py:77
  16.4 0.3 %dots.1 = f32[32,512]{1,0:T(8,128)S(1)} custom-call(bf16[8,1536]{1,0:T(8,128)(2,1)S(1)} %get-tuple-element.26.refs_0_, bf16[8,1536]{1,0:T(8,128)(2,1)S(1)} %collective-permute-done.refs_1_, bf16[8,1536]{1,0:T(8,128)(2,1)S(1)} %collective-permute-done.2.refs_2_, bf16[8,1536]{1,0:T(8,128)(2,1)S(1)} %collective-permute-done.3.refs_3_, ...), custom_call_target="tpu_custom_call" | custom-call | tf_op jit(solution)/shard_map/dots/pallas_call | solution.py:19
  16.8 0.5 %collective-permute-start.10 = (f32[8,512]{1,0:T(8,128)S(1)}, f32[8,512]{1,0:T(8,128)S(1)}, u32[]{:S(2)}, u32[]{:S(2)}) collective-permute-start(f32[8,512]{1,0:T(8,128)S(1)} %get-tuple-element.45), channel_id=1, source_target_pairs={{0,2},{1,3},{2,4},{3,5},{4,6},{5,7},{6,0},{7,1},{8,10},{9,11},{10,... | collective-permute-start | bytes 49160 | tf_op jit(solution)/shard_map/ppermute | solution.py:81
  17.3 2.6 %collective-permute-start.11 = (f32[8,512]{1,0:T(8,128)S(1)}, f32[8,512]{1,0:T(8,128)S(1)}, u32[]{:S(2)}, u32[]{:S(2)}) collective-permute-start(f32[8,512]{1,0:T(8,128)S(1)} %get-tuple-element.47), channel_id=1, source_target_pairs={{0,4},{1,5},{2,6},{3,7},{4,0},{5,1},{6,2},{7,3},{8,12},{9,13},{10,... | collective-permute-start | bytes 49160 | tf_op jit(solution)/shard_map/ppermute | solution.py:81
  19.9 1.6 %collective-permute-start.12 = (f32[8,512]{1,0:T(8,128)S(1)}, f32[8,512]{1,0:T(8,128)S(1)}, u32[]{:S(2)}, u32[]{:S(2)}) collective-permute-start(f32[8,512]{1,0:T(8,128)S(1)} %get-tuple-element.46), channel_id=1, source_target_pairs={{0,6},{1,7},{2,0},{3,1},{4,2},{5,3},{6,4},{7,5},{8,14},{9,15},{10,... | collective-permute-start | bytes 49160 | tf_op jit(solution)/shard_map/ppermute | solution.py:81
  21.5 1.0 %collective-permute-done.10 = f32[8,512]{1,0:T(8,128)S(1)} collective-permute-done((f32[8,512]{1,0:T(8,128)S(1)}, f32[8,512]{1,0:T(8,128)S(1)}, u32[]{:S(2)}, u32[]{:S(2)}) %collective-permute-start.10) | collective-permute-done | bytes 16416 | tf_op jit(solution)/shard_map/ppermute | solution.py:81
  22.6 0.0 collective-permute-done.11
  22.6 1.1 %collective-permute-done.12 = f32[8,512]{1,0:T(8,128)S(1)} collective-permute-done((f32[8,512]{1,0:T(8,128)S(1)}, f32[8,512]{1,0:T(8,128)S(1)}, u32[]{:S(2)}, u32[]{:S(2)}) %collective-permute-start.12) | collective-permute-done | bytes 16416 | tf_op jit(solution)/shard_map/ppermute | solution.py:81
  23.7 0.6 %fusion.2 = bf16[8,512]{1,0:T(8,128)(2,1)} fusion(f32[8,512]{1,0:T(8,128)S(1)} %collective-permute-done.12, f32[8,512]{1,0:T(8,128)S(1)} %collective-permute-done.11, f32[8,512]{1,0:T(8,128)S(1)} %collective-permute-done.10, f32[32,512]{1,0:T(8,128)S(1)} %dots.1), kind=kLoop, calls=%fused_computation.3 | loop fusion | flops 16384 | bytes 73728 | tf_op jit(solution)/shard_map/convert_element_type | solution.py:126
  (2 shorter events, 0.0 us)
Async XLA Ops:
  0.0 3.0 %copy-start = (bf16[768,128]{1,0:T(8,128)(2,1)S(1)}, bf16[768,128]{1,0:T(8,128)(2,1)}, u32[]{:S(2)}) copy-start(bf16[768,128]{1,0:T(8,128)(2,1)} %refs_4_) | copy-start | bytes 589828
  0.0 5.3 %copy-start.1 = (bf16[8,6144]{1,0:T(8,128)(2,1)S(1)}, bf16[8,6144]{1,0:T(8,128)(2,1)}, u32[]{:S(2)}) copy-start(bf16[8,6144]{1,0:T(8,128)(2,1)} %amplitude_ref.1) | copy-start | bytes 294916
  0.0 5.3 %copy-start.2 = (s32[1,48]{1,0:T(1,128)S(1)}, s32[1,48]{1,0:T(1,128)}, u32[]{:S(2)}) copy-start(s32[1,48]{1,0:T(1,128)} %mask_ref.1) | copy-start | bytes 580
  0.0 5.3 %copy-start.3 = (s32[48]{0:T(128)S(1)}, s32[48]{0:T(128)}, u32[]{:S(2)}) copy-start(s32[48]{0:T(128)} %size_ref.1) | copy-start | bytes 580
  0.0 9.7 %collective-permute-start.1 = (bf16[768,128]{1,0:T(8,128)(2,1)}, bf16[768,128]{1,0:T(8,128)(2,1)S(1)}, u32[]{:S(2)}, u32[]{:S(2)}) collective-permute-start(bf16[768,128]{1,0:T(8,128)(2,1)} %refs_4_), channel_id=1, source_target_pairs={{0,8},{8,0},{16,24},{24,16},{1,9},{9,1},{17,25},{25,17},{2,10},{10... | collective-permute-start | bytes 589832 | tf_op jit(solution)/shard_map/ppermute | solution.py:77
  3.0 11.4 %collective-permute-start.4 = (bf16[768,128]{1,0:T(8,128)(2,1)S(1)}, bf16[768,128]{1,0:T(8,128)(2,1)S(1)}, u32[]{:S(2)}, u32[]{:S(2)}) collective-permute-start(bf16[768,128]{1,0:T(8,128)(2,1)S(1)} %copy-done), channel_id=1, source_target_pairs={{0,16},{8,24},{16,0},{24,8},{1,17},{9,25},{17,1},{25,9},{2,18},{10... | collective-permute-start | bytes 589832 | tf_op jit(solution)/shard_map/ppermute | solution.py:77
  4.5 9.9 %collective-permute-start.5 = (bf16[768,128]{1,0:T(8,128)(2,1)S(1)}, bf16[768,128]{1,0:T(8,128)(2,1)S(1)}, u32[]{:S(2)}, u32[]{:S(2)}) collective-permute-start(bf16[768,128]{1,0:T(8,128)(2,1)S(1)} %copy-done), channel_id=1, source_target_pairs={{0,24},{8,16},{16,8},{24,0},{1,25},{9,17},{17,9},{25,1},{2,26},{10... | collective-permute-start | bytes 589832 | tf_op jit(solution)/shard_map/ppermute | solution.py:77
  6.0 5.8 %collective-permute-start = (bf16[8,1536]{1,0:T(8,128)(2,1)S(1)}, bf16[8,1536]{1,0:T(8,128)(2,1)S(1)}, u32[]{:S(2)}, u32[]{:S(2)}) collective-permute-start(bf16[8,1536]{1,0:T(8,128)(2,1)S(1)} %get-tuple-element.27), channel_id=1, source_target_pairs={{0,6},{1,7},{2,4},{3,5},{4,2},{5,3},{6,0},{7,1},{8,14},{9,15},{10,... | collective-permute-start | bytes 73736 | tf_op jit(solution)/shard_map/ppermute | solution.py:77
  9.7 4.7 %collective-permute-start.2 = (bf16[8,1536]{1,0:T(8,128)(2,1)S(1)}, bf16[8,1536]{1,0:T(8,128)(2,1)S(1)}, u32[]{:S(2)}, u32[]{:S(2)}) collective-permute-start(bf16[8,1536]{1,0:T(8,128)(2,1)S(1)} %get-tuple-element.32), channel_id=1, source_target_pairs={{0,4},{1,5},{2,6},{3,7},{4,0},{5,1},{6,2},{7,3},{8,12},{9,13},{10,... | collective-permute-start | bytes 73736 | tf_op jit(solution)/shard_map/ppermute | solution.py:77
  9.7 4.7 %collective-permute-start.3 = (bf16[8,1536]{1,0:T(8,128)(2,1)S(1)}, bf16[8,1536]{1,0:T(8,128)(2,1)S(1)}, u32[]{:S(2)}, u32[]{:S(2)}) collective-permute-start(bf16[8,1536]{1,0:T(8,128)(2,1)S(1)} %get-tuple-element.33), channel_id=1, source_target_pairs={{0,2},{1,3},{2,0},{3,1},{4,6},{5,7},{6,4},{7,5},{8,10},{9,11},{10,... | collective-permute-start | bytes 73736 | tf_op jit(solution)/shard_map/ppermute | solution.py:77
  11.8 3.3 %collective-permute-start.6 = (bf16[768,128]{1,0:T(8,128)(2,1)S(1)}, bf16[768,128]{1,0:T(8,128)(2,1)S(1)}, u32[]{:S(2)}, u32[]{:S(2)}) collective-permute-start(bf16[768,128]{1,0:T(8,128)(2,1)S(1)} %copy-done), channel_id=1, source_target_pairs={{0,1},{1,0},{2,3},{3,2},{4,5},{5,4},{6,7},{7,6},{8,9},{9,8},{10,11... | collective-permute-start | bytes 589832 | tf_op jit(solution)/shard_map/ppermute | solution.py:77
  14.4 1.4 %collective-permute-start.7 = (bf16[768,128]{1,0:T(8,128)(2,1)S(1)}, bf16[768,128]{1,0:T(8,128)(2,1)S(1)}, u32[]{:S(2)}, u32[]{:S(2)}) collective-permute-start(bf16[768,128]{1,0:T(8,128)(2,1)S(1)} %collective-permute-done.1.refs_5_), channel_id=1, source_target_pairs={{0,1},{1,0},{2,3},{3,2},{4,5},{5,4},{6,7},{7,6},{8,9},{9,8},{10,11... | collective-permute-start | bytes 589832 | tf_op jit(solution)/shard_map/ppermute | solution.py:77
  14.4 1.7 %collective-permute-start.9 = (bf16[768,128]{1,0:T(8,128)(2,1)S(1)}, bf16[768,128]{1,0:T(8,128)(2,1)S(1)}, u32[]{:S(2)}, u32[]{:S(2)}) collective-permute-start(bf16[768,128]{1,0:T(8,128)(2,1)S(1)} %collective-permute-done.5.refs_7_), channel_id=1, source_target_pairs={{0,1},{1,0},{2,3},{3,2},{4,5},{5,4},{6,7},{7,6},{8,9},{9,8},{10,11... | collective-permute-start | bytes 589832 | tf_op jit(solution)/shard_map/ppermute | solution.py:77
  15.0 1.4 %collective-permute-start.8 = (bf16[768,128]{1,0:T(8,128)(2,1)S(1)}, bf16[768,128]{1,0:T(8,128)(2,1)S(1)}, u32[]{:S(2)}, u32[]{:S(2)}) collective-permute-start(bf16[768,128]{1,0:T(8,128)(2,1)S(1)} %collective-permute-done.4.refs_6_), channel_id=1, source_target_pairs={{0,1},{1,0},{2,3},{3,2},{4,5},{5,4},{6,7},{7,6},{8,9},{9,8},{10,11... | collective-permute-start | bytes 589832 | tf_op jit(solution)/shard_map/ppermute | solution.py:77
  16.8 5.7 %collective-permute-start.10 = (f32[8,512]{1,0:T(8,128)S(1)}, f32[8,512]{1,0:T(8,128)S(1)}, u32[]{:S(2)}, u32[]{:S(2)}) collective-permute-start(f32[8,512]{1,0:T(8,128)S(1)} %get-tuple-element.45), channel_id=1, source_target_pairs={{0,2},{1,3},{2,4},{3,5},{4,6},{5,7},{6,0},{7,1},{8,10},{9,11},{10,... | collective-permute-start | bytes 49160 | tf_op jit(solution)/shard_map/ppermute | solution.py:81
  17.3 5.2 %collective-permute-start.11 = (f32[8,512]{1,0:T(8,128)S(1)}, f32[8,512]{1,0:T(8,128)S(1)}, u32[]{:S(2)}, u32[]{:S(2)}) collective-permute-start(f32[8,512]{1,0:T(8,128)S(1)} %get-tuple-element.47), channel_id=1, source_target_pairs={{0,4},{1,5},{2,6},{3,7},{4,0},{5,1},{6,2},{7,3},{8,12},{9,13},{10,... | collective-permute-start | bytes 49160 | tf_op jit(solution)/shard_map/ppermute | solution.py:81
  19.9 3.7 %collective-permute-start.12 = (f32[8,512]{1,0:T(8,128)S(1)}, f32[8,512]{1,0:T(8,128)S(1)}, u32[]{:S(2)}, u32[]{:S(2)}) collective-permute-start(f32[8,512]{1,0:T(8,128)S(1)} %get-tuple-element.46), channel_id=1, source_target_pairs={{0,6},{1,7},{2,0},{3,1},{4,2},{5,3},{6,4},{7,5},{8,14},{9,15},{10,... | collective-permute-start | bytes 49160 | tf_op jit(solution)/shard_map/ppermute | solution.py:81

commit v4 on v3

--- a/solution.py
+++ b/solution.py
@@ -76,8 +76,11 @@
     def swap(array, axis, size, step):
         return lax.ppermute(array, axis, [(k, k ^ step) for k in range(size)])
 
+    ring = [k ^ (k >> 1) for k in range(chips)]
+    after_chip = [[ring[(ring.index(k) + step) % chips] for k in range(chips)] for step in range(chips)]
+
     def shift(array, step):
-        pairs = [(k, (k // CORES + step) % chips * CORES + k % CORES) for k in range(grp_size)]
+        pairs = [(k, after_chip[step][k // CORES] * CORES + k % CORES) for k in range(grp_size)]
         return lax.ppermute(array, "grp", pairs)
 
     lane = local_call(
@@ -92,10 +95,10 @@
     lane, later = lax.optimization_barrier((lane, integrals))
     own = [integrals] + [swap(integrals if step == 1 else later, "blk", blk_size, step) for step in range(1, blk_size)]
 
-    order = (0, *range(chips - 1, 0, -1))
+    order = sorted(range(chips), key=lambda step: (step != 0, step != chips // 2, -step))
     block = jax.ShapeDtypeStruct((rows, CORES * depth), amplitudes.dtype)
     blocks = local_call(
-        functools.partial(mask_kernel, order),
+        functools.partial(mask_kernel, tuple(order)),
         "live_blocks",
         [block] * chips,
         [VMEM, SMEM, SMEM, VMEM],
@@ -121,7 +124,9 @@
     )
     ladder = partial[:rows]
     for step in range(1, chips):
-        place = chips - (chip ^ lax.rem(chip + step, chips))
+        place = 0
+        for k in range(chips):
+            place = jnp.where(chip == k, order.index(k ^ after_chip[step][k]), place)
         ladder += shift(lax.dynamic_slice_in_dim(partial, place * rows, rows), step)
     return ladder.astype(jnp.bfloat16)
 

time: 24.4 us -> 24.3 us (level)
  transfers between devices with their start and end apart: 13 -> 13, of which waited for: 7 -> 6; matrix products, arithmetic and copies ran while one was open for 0% -> 0% of each run, Pallas kernels for 3% -> 3%
where the time goes in v4:
time: 24.3 us; the launch traced here: 24.1 us
  starting transfers between devices  15.7 us (65%)
  waiting for transfers between devices  6.73 us (28%)
  Pallas kernels  1.02 us (4%)
  other arithmetic  0.61 us (3%)
    ppermute x10, starting transfers between devices, swap(): return lax.ppermute(array, axis, [(k, k ^ step) for k in range(size)])  11 us
    ppermute x3, starting transfers between devices, shift(): return lax.ppermute(array, 'grp', pairs)  4.67 us
    ppermute x10, waiting for transfers between devices, swap(): return lax.ppermute(array, axis, [(k, k ^ step) for k in range(size)])  4.56 us
    ppermute x3, waiting for transfers between devices, shift(): return lax.ppermute(array, 'grp', pairs)  2.16 us
    pallas_call x3, Pallas kernels, local_call(): pl.pallas_call(kernel, out_shape=out_shape, in_specs=in_specs, out_specs=...  1.02 us
    convert_element_type x1, other arithmetic, body(): return ladder.astype(jnp.bfloat16)  0.61 us
  transfers between devices with their start and end apart: 13, of which 6 were waited for; matrix products, arithmetic and copies ran while one was open for 0% of the time, Pallas kernels for 3%

profile of v4, /device:TPU:0, one launch (start us, length us, event | category | flops | bytes accessed | tf_op | source)
XLA Modules:
  0.0 24.1 jit_solution(54911899318028654)
XLA Ops:
  0.0 0.0 copy-start
  0.0 0.0 copy-start.1
  0.0 0.0 copy-start.2
  0.0 0.0 copy-start.3
  0.0 3.0 %collective-permute-start.1 = (bf16[768,128]{1,0:T(8,128)(2,1)}, bf16[768,128]{1,0:T(8,128)(2,1)S(1)}, u32[]{:S(2)}, u32[]{:S(2)}) collective-permute-start(bf16[768,128]{1,0:T(8,128)(2,1)} %refs_4_), channel_id=1, source_target_pairs={{0,8},{8,0},{16,24},{24,16},{1,9},{9,1},{17,25},{25,17},{2,10},{10... | collective-permute-start | bytes 589832 | tf_op jit(solution)/shard_map/ppermute | solution.py:77
  3.0 0.0 copy-done
  3.0 1.5 %collective-permute-start.4 = (bf16[768,128]{1,0:T(8,128)(2,1)S(1)}, bf16[768,128]{1,0:T(8,128)(2,1)S(1)}, u32[]{:S(2)}, u32[]{:S(2)}) collective-permute-start(bf16[768,128]{1,0:T(8,128)(2,1)S(1)} %copy-done), channel_id=1, source_target_pairs={{0,16},{8,24},{16,0},{24,8},{1,17},{9,25},{17,1},{25,9},{2,18},{10... | collective-permute-start | bytes 589832 | tf_op jit(solution)/shard_map/ppermute | solution.py:77
  4.5 0.8 %collective-permute-start.5 = (bf16[768,128]{1,0:T(8,128)(2,1)S(1)}, bf16[768,128]{1,0:T(8,128)(2,1)S(1)}, u32[]{:S(2)}, u32[]{:S(2)}) collective-permute-start(bf16[768,128]{1,0:T(8,128)(2,1)S(1)} %copy-done), channel_id=1, source_target_pairs={{0,24},{8,16},{16,8},{24,0},{1,25},{9,17},{17,9},{25,1},{2,26},{10... | collective-permute-start | bytes 589832 | tf_op jit(solution)/shard_map/ppermute | solution.py:77
  5.3 0.0 copy-done.1
  5.3 0.0 copy-done.2
  5.3 0.0 copy-done.3
  5.3 0.7 %live_blocks.1 = (bf16[8,1536]{1,0:T(8,128)(2,1)S(1)}, bf16[8,1536]{1,0:T(8,128)(2,1)S(1)}, bf16[8,1536]{1,0:T(8,128)(2,1)S(1)}, bf16[8,1536]{1,0:T(8,128)(2,1)S(1)}) custom-call(s32[8,128]{1,0:T(8,128)S(1)} %lane.1.lane_ref, s32[1,48]{1,0:T(1,128)S(1)} %copy-done.2, s32[48]{0:T(128)S(1)} %copy-done.3, bf16[8,6144]{1,0:T(8,128)(2,1)S(1)} %copy-done.1), custom_call_target="tpu_custom_call" | custom-call | tf_op jit(solution)/shard_map/live_blocks/pallas_call | solution.py:19
  6.0 2.7 %collective-permute-start = (bf16[8,1536]{1,0:T(8,128)(2,1)S(1)}, bf16[8,1536]{1,0:T(8,128)(2,1)S(1)}, u32[]{:S(2)}, u32[]{:S(2)}) collective-permute-start(bf16[8,1536]{1,0:T(8,128)(2,1)S(1)} %get-tuple-element.27), channel_id=1, source_target_pairs={{0,4},{1,5},{2,6},{3,7},{4,0},{5,1},{6,2},{7,3},{8,12},{9,13},{10,... | collective-permute-start | bytes 73736 | tf_op jit(solution)/shard_map/ppermute | solution.py:77
  8.7 1.3 %collective-permute-start.2 = (bf16[8,1536]{1,0:T(8,128)(2,1)S(1)}, bf16[8,1536]{1,0:T(8,128)(2,1)S(1)}, u32[]{:S(2)}, u32[]{:S(2)}) collective-permute-start(bf16[8,1536]{1,0:T(8,128)(2,1)S(1)} %get-tuple-element.32), channel_id=1, source_target_pairs={{0,6},{1,7},{2,4},{3,5},{4,2},{5,3},{6,0},{7,1},{8,14},{9,15},{10,... | collective-permute-start | bytes 73736 | tf_op jit(solution)/shard_map/ppermute | solution.py:77
  10.0 0.0 collective-permute-done.1.refs_5_
  10.0 1.1 %collective-permute-start.3 = (bf16[8,1536]{1,0:T(8,128)(2,1)S(1)}, bf16[8,1536]{1,0:T(8,128)(2,1)S(1)}, u32[]{:S(2)}, u32[]{:S(2)}) collective-permute-start(bf16[8,1536]{1,0:T(8,128)(2,1)S(1)} %get-tuple-element.33), channel_id=1, source_target_pairs={{0,2},{1,3},{2,0},{3,1},{4,6},{5,7},{6,4},{7,5},{8,10},{9,11},{10,... | collective-permute-start | bytes 73736 | tf_op jit(solution)/shard_map/ppermute | solution.py:77
  11.1 0.0 collective-permute-done.refs_1_
  11.1 0.0 collective-permute-start.6
  11.1 3.2 %collective-permute-done.2.refs_2_ = bf16[8,1536]{1,0:T(8,128)(2,1)S(1)} collective-permute-done((bf16[8,1536]{1,0:T(8,128)(2,1)S(1)}, bf16[8,1536]{1,0:T(8,128)(2,1)S(1)}, u32[]{:S(2)}, u32[]{:S(2)}) %collective-permute-start.2) | collective-permute-done | bytes 24608 | tf_op jit(solution)/shard_map/ppermute | solution.py:77
  14.3 0.0 collective-permute-start.7
  14.3 0.0 collective-permute-done.4.refs_6_
  14.3 0.0 collective-permute-done.3.refs_3_
  14.3 0.0 collective-permute-done.5.refs_7_
  14.3 0.6 %collective-permute-start.9 = (bf16[768,128]{1,0:T(8,128)(2,1)S(1)}, bf16[768,128]{1,0:T(8,128)(2,1)S(1)}, u32[]{:S(2)}, u32[]{:S(2)}) collective-permute-start(bf16[768,128]{1,0:T(8,128)(2,1)S(1)} %collective-permute-done.5.refs_7_), channel_id=1, source_target_pairs={{0,1},{1,0},{2,3},{3,2},{4,5},{5,4},{6,7},{7,6},{8,9},{9,8},{10,11... | collective-permute-start | bytes 589832 | tf_op jit(solution)/shard_map/ppermute | solution.py:77
  14.9 0.1 collective-permute-start.8
  15.0 0.0 collective-permute-done.6.refs_8_
  15.0 0.8 %collective-permute-done.7.refs_9_ = bf16[768,128]{1,0:T(8,128)(2,1)S(1)} collective-permute-done((bf16[768,128]{1,0:T(8,128)(2,1)S(1)}, bf16[768,128]{1,0:T(8,128)(2,1)S(1)}, u32[]{:S(2)}, u32[]{:S(2)}) %collective-permute-start.7) | collective-permute-done | bytes 196640 | tf_op jit(solution)/shard_map/ppermute | solution.py:77
  15.7 0.3 %collective-permute-done.9.refs_11_ = bf16[768,128]{1,0:T(8,128)(2,1)S(1)} collective-permute-done((bf16[768,128]{1,0:T(8,128)(2,1)S(1)}, bf16[768,128]{1,0:T(8,128)(2,1)S(1)}, u32[]{:S(2)}, u32[]{:S(2)}) %collective-permute-start.9) | collective-permute-done | bytes 196640 | tf_op jit(solution)/shard_map/ppermute | solution.py:77
  16.0 0.3 %collective-permute-done.8.refs_10_ = bf16[768,128]{1,0:T(8,128)(2,1)S(1)} collective-permute-done((bf16[768,128]{1,0:T(8,128)(2,1)S(1)}, bf16[768,128]{1,0:T(8,128)(2,1)S(1)}, u32[]{:S(2)}, u32[]{:S(2)}) %collective-permute-start.8) | collective-permute-done | bytes 196640 | tf_op jit(solution)/shard_map/ppermute | solution.py:77
  16.3 0.3 %dots.1 = f32[32,512]{1,0:T(8,128)S(1)} custom-call(bf16[8,1536]{1,0:T(8,128)(2,1)S(1)} %get-tuple-element.26.refs_0_, bf16[8,1536]{1,0:T(8,128)(2,1)S(1)} %collective-permute-done.refs_1_, bf16[8,1536]{1,0:T(8,128)(2,1)S(1)} %collective-permute-done.2.refs_2_, bf16[8,1536]{1,0:T(8,128)(2,1)S(1)} %collective-permute-done.3.refs_3_, ...), custom_call_target="tpu_custom_call" | custom-call | tf_op jit(solution)/shard_map/dots/pallas_call | solution.py:19
  16.7 0.6 %collective-permute-start.10 = (f32[8,512]{1,0:T(8,128)S(1)}, f32[8,512]{1,0:T(8,128)S(1)}, u32[]{:S(2)}, u32[]{:S(2)}) collective-permute-start(f32[8,512]{1,0:T(8,128)S(1)} %get-tuple-element.45), channel_id=1, source_target_pairs={{0,2},{1,3},{2,6},{3,7},{4,0},{5,1},{6,4},{7,5},{8,10},{9,11},{10,... | collective-permute-start | bytes 49160 | tf_op jit(solution)/shard_map/ppermute | solution.py:84
  17.3 2.5 %collective-permute-start.11 = (f32[8,512]{1,0:T(8,128)S(1)}, f32[8,512]{1,0:T(8,128)S(1)}, u32[]{:S(2)}, u32[]{:S(2)}) collective-permute-start(f32[8,512]{1,0:T(8,128)S(1)} %get-tuple-element.47), channel_id=1, source_target_pairs={{0,6},{1,7},{2,4},{3,5},{4,2},{5,3},{6,0},{7,1},{8,14},{9,15},{10,... | collective-permute-start | bytes 49160 | tf_op jit(solution)/shard_map/ppermute | solution.py:84
  19.8 1.6 %collective-permute-start.12 = (f32[8,512]{1,0:T(8,128)S(1)}, f32[8,512]{1,0:T(8,128)S(1)}, u32[]{:S(2)}, u32[]{:S(2)}) collective-permute-start(f32[8,512]{1,0:T(8,128)S(1)} %get-tuple-element.46), channel_id=1, source_target_pairs={{0,4},{1,5},{2,0},{3,1},{4,6},{5,7},{6,2},{7,3},{8,12},{9,13},{10,... | collective-permute-start | bytes 49160 | tf_op jit(solution)/shard_map/ppermute | solution.py:84
  21.4 0.0 collective-permute-done.10
  21.4 1.5 %collective-permute-done.11 = f32[8,512]{1,0:T(8,128)S(1)} collective-permute-done((f32[8,512]{1,0:T(8,128)S(1)}, f32[8,512]{1,0:T(8,128)S(1)}, u32[]{:S(2)}, u32[]{:S(2)}) %collective-permute-start.11) | collective-permute-done | bytes 16416 | tf_op jit(solution)/shard_map/ppermute | solution.py:84
  22.9 0.7 %collective-permute-done.12 = f32[8,512]{1,0:T(8,128)S(1)} collective-permute-done((f32[8,512]{1,0:T(8,128)S(1)}, f32[8,512]{1,0:T(8,128)S(1)}, u32[]{:S(2)}, u32[]{:S(2)}) %collective-permute-start.12) | collective-permute-done | bytes 16416 | tf_op jit(solution)/shard_map/ppermute | solution.py:84
  23.5 0.6 %fusion.2 = bf16[8,512]{1,0:T(8,128)(2,1)} fusion(f32[8,512]{1,0:T(8,128)S(1)} %collective-permute-done.12, f32[8,512]{1,0:T(8,128)S(1)} %collective-permute-done.11, f32[8,512]{1,0:T(8,128)S(1)} %collective-permute-done.10, f32[32,512]{1,0:T(8,128)S(1)} %dots.1), kind=kLoop, calls=%fused_computation.3 | loop fusion | flops 16384 | bytes 73728 | tf_op jit(solution)/shard_map/convert_element_type | solution.py:131
  (2 shorter events, 0.0 us)
Async XLA Ops:
  0.0 3.0 %copy-start = (bf16[768,128]{1,0:T(8,128)(2,1)S(1)}, bf16[768,128]{1,0:T(8,128)(2,1)}, u32[]{:S(2)}) copy-start(bf16[768,128]{1,0:T(8,128)(2,1)} %refs_4_) | copy-start | bytes 589828
  0.0 5.3 %copy-start.1 = (bf16[8,6144]{1,0:T(8,128)(2,1)S(1)}, bf16[8,6144]{1,0:T(8,128)(2,1)}, u32[]{:S(2)}) copy-start(bf16[8,6144]{1,0:T(8,128)(2,1)} %amplitude_ref.1) | copy-start | bytes 294916
  0.0 5.3 %copy-start.2 = (s32[1,48]{1,0:T(1,128)S(1)}, s32[1,48]{1,0:T(1,128)}, u32[]{:S(2)}) copy-start(s32[1,48]{1,0:T(1,128)} %mask_ref.1) | copy-start | bytes 580
  0.0 5.3 %copy-start.3 = (s32[48]{0:T(128)S(1)}, s32[48]{0:T(128)}, u32[]{:S(2)}) copy-start(s32[48]{0:T(128)} %size_ref.1) | copy-start | bytes 580
  0.0 10.0 %collective-permute-start.1 = (bf16[768,128]{1,0:T(8,128)(2,1)}, bf16[768,128]{1,0:T(8,128)(2,1)S(1)}, u32[]{:S(2)}, u32[]{:S(2)}) collective-permute-start(bf16[768,128]{1,0:T(8,128)(2,1)} %refs_4_), channel_id=1, source_target_pairs={{0,8},{8,0},{16,24},{24,16},{1,9},{9,1},{17,25},{25,17},{2,10},{10... | collective-permute-start | bytes 589832 | tf_op jit(solution)/shard_map/ppermute | solution.py:77
  3.0 11.3 %collective-permute-start.4 = (bf16[768,128]{1,0:T(8,128)(2,1)S(1)}, bf16[768,128]{1,0:T(8,128)(2,1)S(1)}, u32[]{:S(2)}, u32[]{:S(2)}) collective-permute-start(bf16[768,128]{1,0:T(8,128)(2,1)S(1)} %copy-done), channel_id=1, source_target_pairs={{0,16},{8,24},{16,0},{24,8},{1,17},{9,25},{17,1},{25,9},{2,18},{10... | collective-permute-start | bytes 589832 | tf_op jit(solution)/shard_map/ppermute | solution.py:77
  4.5 9.8 %collective-permute-start.5 = (bf16[768,128]{1,0:T(8,128)(2,1)S(1)}, bf16[768,128]{1,0:T(8,128)(2,1)S(1)}, u32[]{:S(2)}, u32[]{:S(2)}) collective-permute-start(bf16[768,128]{1,0:T(8,128)(2,1)S(1)} %copy-done), channel_id=1, source_target_pairs={{0,24},{8,16},{16,8},{24,0},{1,25},{9,17},{17,9},{25,1},{2,26},{10... | collective-permute-start | bytes 589832 | tf_op jit(solution)/shard_map/ppermute | solution.py:77
  6.0 5.1 %collective-permute-start = (bf16[8,1536]{1,0:T(8,128)(2,1)S(1)}, bf16[8,1536]{1,0:T(8,128)(2,1)S(1)}, u32[]{:S(2)}, u32[]{:S(2)}) collective-permute-start(bf16[8,1536]{1,0:T(8,128)(2,1)S(1)} %get-tuple-element.27), channel_id=1, source_target_pairs={{0,4},{1,5},{2,6},{3,7},{4,0},{5,1},{6,2},{7,3},{8,12},{9,13},{10,... | collective-permute-start | bytes 73736 | tf_op jit(solution)/shard_map/ppermute | solution.py:77
  8.7 5.6 %collective-permute-start.2 = (bf16[8,1536]{1,0:T(8,128)(2,1)S(1)}, bf16[8,1536]{1,0:T(8,128)(2,1)S(1)}, u32[]{:S(2)}, u32[]{:S(2)}) collective-permute-start(bf16[8,1536]{1,0:T(8,128)(2,1)S(1)} %get-tuple-element.32), channel_id=1, source_target_pairs={{0,6},{1,7},{2,4},{3,5},{4,2},{5,3},{6,0},{7,1},{8,14},{9,15},{10,... | collective-permute-start | bytes 73736 | tf_op jit(solution)/shard_map/ppermute | solution.py:77
  10.0 4.3 %collective-permute-start.3 = (bf16[8,1536]{1,0:T(8,128)(2,1)S(1)}, bf16[8,1536]{1,0:T(8,128)(2,1)S(1)}, u32[]{:S(2)}, u32[]{:S(2)}) collective-permute-start(bf16[8,1536]{1,0:T(8,128)(2,1)S(1)} %get-tuple-element.33), channel_id=1, source_target_pairs={{0,2},{1,3},{2,0},{3,1},{4,6},{5,7},{6,4},{7,5},{8,10},{9,11},{10,... | collective-permute-start | bytes 73736 | tf_op jit(solution)/shard_map/ppermute | solution.py:77
  11.1 3.9 %collective-permute-start.6 = (bf16[768,128]{1,0:T(8,128)(2,1)S(1)}, bf16[768,128]{1,0:T(8,128)(2,1)S(1)}, u32[]{:S(2)}, u32[]{:S(2)}) collective-permute-start(bf16[768,128]{1,0:T(8,128)(2,1)S(1)} %copy-done), channel_id=1, source_target_pairs={{0,1},{1,0},{2,3},{3,2},{4,5},{5,4},{6,7},{7,6},{8,9},{9,8},{10,11... | collective-permute-start | bytes 589832 | tf_op jit(solution)/shard_map/ppermute | solution.py:77
  14.3 1.4 %collective-permute-start.7 = (bf16[768,128]{1,0:T(8,128)(2,1)S(1)}, bf16[768,128]{1,0:T(8,128)(2,1)S(1)}, u32[]{:S(2)}, u32[]{:S(2)}) collective-permute-start(bf16[768,128]{1,0:T(8,128)(2,1)S(1)} %collective-permute-done.1.refs_5_), channel_id=1, source_target_pairs={{0,1},{1,0},{2,3},{3,2},{4,5},{5,4},{6,7},{7,6},{8,9},{9,8},{10,11... | collective-permute-start | bytes 589832 | tf_op jit(solution)/shard_map/ppermute | solution.py:77
  14.3 1.7 %collective-permute-start.9 = (bf16[768,128]{1,0:T(8,128)(2,1)S(1)}, bf16[768,128]{1,0:T(8,128)(2,1)S(1)}, u32[]{:S(2)}, u32[]{:S(2)}) collective-permute-start(bf16[768,128]{1,0:T(8,128)(2,1)S(1)} %collective-permute-done.5.refs_7_), channel_id=1, source_target_pairs={{0,1},{1,0},{2,3},{3,2},{4,5},{5,4},{6,7},{7,6},{8,9},{9,8},{10,11... | collective-permute-start | bytes 589832 | tf_op jit(solution)/shard_map/ppermute | solution.py:77
  14.9 1.4 %collective-permute-start.8 = (bf16[768,128]{1,0:T(8,128)(2,1)S(1)}, bf16[768,128]{1,0:T(8,128)(2,1)S(1)}, u32[]{:S(2)}, u32[]{:S(2)}) collective-permute-start(bf16[768,128]{1,0:T(8,128)(2,1)S(1)} %collective-permute-done.4.refs_6_), channel_id=1, source_target_pairs={{0,1},{1,0},{2,3},{3,2},{4,5},{5,4},{6,7},{7,6},{8,9},{9,8},{10,11... | collective-permute-start | bytes 589832 | tf_op jit(solution)/shard_map/ppermute | solution.py:77
  16.7 4.7 %collective-permute-start.10 = (f32[8,512]{1,0:T(8,128)S(1)}, f32[8,512]{1,0:T(8,128)S(1)}, u32[]{:S(2)}, u32[]{:S(2)}) collective-permute-start(f32[8,512]{1,0:T(8,128)S(1)} %get-tuple-element.45), channel_id=1, source_target_pairs={{0,2},{1,3},{2,6},{3,7},{4,0},{5,1},{6,4},{7,5},{8,10},{9,11},{10,... | collective-permute-start | bytes 49160 | tf_op jit(solution)/shard_map/ppermute | solution.py:84
  17.3 5.5 %collective-permute-start.11 = (f32[8,512]{1,0:T(8,128)S(1)}, f32[8,512]{1,0:T(8,128)S(1)}, u32[]{:S(2)}, u32[]{:S(2)}) collective-permute-start(f32[8,512]{1,0:T(8,128)S(1)} %get-tuple-element.47), channel_id=1, source_target_pairs={{0,6},{1,7},{2,4},{3,5},{4,2},{5,3},{6,0},{7,1},{8,14},{9,15},{10,... | collective-permute-start | bytes 49160 | tf_op jit(solution)/shard_map/ppermute | solution.py:84
  19.8 3.7 %collective-permute-start.12 = (f32[8,512]{1,0:T(8,128)S(1)}, f32[8,512]{1,0:T(8,128)S(1)}, u32[]{:S(2)}, u32[]{:S(2)}) collective-permute-start(f32[8,512]{1,0:T(8,128)S(1)} %get-tuple-element.46), channel_id=1, source_target_pairs={{0,4},{1,5},{2,0},{3,1},{4,6},{5,7},{6,2},{7,3},{8,12},{9,13},{10,... | collective-permute-start | bytes 49160 | tf_op jit(solution)/shard_map/ppermute | solution.py:84

commit v5 on v4

--- a/solution.py
+++ b/solution.py
@@ -48,16 +48,22 @@
                 out_ref[:, place : place + tile] = jnp.where(lane < live, value, jnp.zeros_like(value))
 
 
-def dot_kernel(members, blocks, *refs):
-    live_refs, own_refs, other_refs = refs[:members], refs[members : members + blocks], refs[members + blocks : -1]
+def dot_kernel(members, first, blocks, early, *refs):
+    live_refs, own_refs, other_refs = refs[:members], refs[members : members + blocks], refs[members + blocks :][:blocks]
     out_ref = refs[-1]
     blk = lax.axis_index("blk")
     depth, cols = own_refs[0].shape
     live = jnp.concatenate([ref[...] for ref in live_refs], axis=0)
-    for step, (own_ref, other_ref) in enumerate(zip(own_refs, other_refs)):
+    for k in range(first if early is False else 0):
+        place = pl.ds(pl.multiple_of((blk ^ k) * cols, cols), cols)
+        out_ref[:, place] = refs[-2][:, k * cols : (k + 1) * cols]
+    for step, (own_ref, other_ref) in enumerate(zip(own_refs, other_refs), first):
         total = jnp.dot(live[:, :depth], own_ref[...], preferred_element_type=jnp.float32)
         total += jnp.dot(live[:, depth:], other_ref[...], preferred_element_type=jnp.float32)
-        out_ref[:, pl.ds(pl.multiple_of((blk ^ step) * cols, cols), cols)] = total
+        if early:
+            out_ref[:, step * cols : (step + 1) * cols] = total
+        else:
+            out_ref[:, pl.ds(pl.multiple_of((blk ^ step) * cols, cols), cols)] = total
 
 
 def after(received, places, value):
@@ -115,12 +121,22 @@
         own[step] = after(received, places, own[step])
         other.append(swap(own[step], "grp", grp_size, 1))
 
+    first = blk_size // 2
+    shape = lambda count: jax.ShapeDtypeStruct((chips * rows, count * cols), jnp.float32)
+    head = local_call(
+        functools.partial(dot_kernel, chips, 0, first, True),
+        "dots_first",
+        shape(first),
+        [VMEM] * (chips + 2 * first),
+        [*received, *own[:first], *other[:first]],
+    )
+    rest = blk_size - first
     partial = local_call(
-        functools.partial(dot_kernel, chips, blk_size),
-        "dots",
-        jax.ShapeDtypeStruct((chips * rows, blk_size * cols), jnp.float32),
-        [VMEM] * (chips + 2 * blk_size),
-        [*received, *own, *other],
+        functools.partial(dot_kernel, chips, first, rest, False),
+        "dots_rest",
+        shape(blk_size),
+        [VMEM] * (chips + 2 * rest + 1),
+        [*received, *own[first:], *other[first:], head],
     )
     ladder = partial[:rows]
     for step in range(1, chips):

time: 24.3 us -> 24.2 us (level)
    pallas_call x3 -> x4, Pallas kernels: 1.02 us -> 1.15 us  [local_call(): pl.pallas_call(kernel, out_shape=out_shape, in_specs=in_specs, out_specs=...]
  transfers between devices with their start and end apart: 13 -> 13, of which waited for: 6 -> 5; matrix products, arithmetic and copies ran while one was open for 0% -> 0% of each run, Pallas kernels for 3% -> 4%
where the time goes in v5:
time: 24.2 us; the launch traced here: 24 us
  starting transfers between devices  15.7 us (65%)
  waiting for transfers between devices  6.49 us (27%)
  Pallas kernels  1.15 us (5%)
  other arithmetic  0.61 us (3%)
    ppermute x10, starting transfers between devices, swap(): return lax.ppermute(array, axis, [(k, k ^ step) for k in range(size)])  11 us
    ppermute x3, starting transfers between devices, shift(): return lax.ppermute(array, 'grp', pairs)  4.67 us
    ppermute x10, waiting for transfers between devices, swap(): return lax.ppermute(array, axis, [(k, k ^ step) for k in range(size)])  4.33 us
    ppermute x3, waiting for transfers between devices, shift(): return lax.ppermute(array, 'grp', pairs)  2.16 us
    pallas_call x4, Pallas kernels, local_call(): pl.pallas_call(kernel, out_shape=out_shape, in_specs=in_specs, out_specs=...  1.15 us
    convert_element_type x1, other arithmetic, body(): return ladder.astype(jnp.bfloat16)  0.61 us
  transfers between devices with their start and end apart: 13, of which 5 were waited for; matrix products, arithmetic and copies ran while one was open for 0% of the time, Pallas kernels for 4%

profile of v5, /device:TPU:0, one launch (start us, length us, event | category | flops | bytes accessed | tf_op | source)
XLA Modules:
  0.0 24.0 jit_solution(7043939111435203488)
XLA Ops:
  0.0 0.0 copy-start
  0.0 0.0 copy-start.1
  0.0 0.0 copy-start.2
  0.0 0.0 copy-start.3
  0.0 3.0 %collective-permute-start.1 = (bf16[768,128]{1,0:T(8,128)(2,1)}, bf16[768,128]{1,0:T(8,128)(2,1)S(1)}, u32[]{:S(2)}, u32[]{:S(2)}) collective-permute-start(bf16[768,128]{1,0:T(8,128)(2,1)} %refs_4_), channel_id=1, source_target_pairs={{0,8},{8,0},{16,24},{24,16},{1,9},{9,1},{17,25},{25,17},{2,10},{10... | collective-permute-start | bytes 589832 | tf_op jit(solution)/shard_map/ppermute | solution.py:83
  3.0 0.0 copy-done
  3.0 1.5 %collective-permute-start.4 = (bf16[768,128]{1,0:T(8,128)(2,1)S(1)}, bf16[768,128]{1,0:T(8,128)(2,1)S(1)}, u32[]{:S(2)}, u32[]{:S(2)}) collective-permute-start(bf16[768,128]{1,0:T(8,128)(2,1)S(1)} %copy-done), channel_id=1, source_target_pairs={{0,16},{8,24},{16,0},{24,8},{1,17},{9,25},{17,1},{25,9},{2,18},{10... | collective-permute-start | bytes 589832 | tf_op jit(solution)/shard_map/ppermute | solution.py:83
  4.5 0.8 %collective-permute-start.5 = (bf16[768,128]{1,0:T(8,128)(2,1)S(1)}, bf16[768,128]{1,0:T(8,128)(2,1)S(1)}, u32[]{:S(2)}, u32[]{:S(2)}) collective-permute-start(bf16[768,128]{1,0:T(8,128)(2,1)S(1)} %copy-done), channel_id=1, source_target_pairs={{0,24},{8,16},{16,8},{24,0},{1,25},{9,17},{17,9},{25,1},{2,26},{10... | collective-permute-start | bytes 589832 | tf_op jit(solution)/shard_map/ppermute | solution.py:83
  5.3 0.0 copy-done.1
  5.3 0.0 copy-done.2
  5.3 0.0 copy-done.3
  5.3 0.7 %live_blocks.1 = (bf16[8,1536]{1,0:T(8,128)(2,1)S(1)}, bf16[8,1536]{1,0:T(8,128)(2,1)S(1)}, bf16[8,1536]{1,0:T(8,128)(2,1)S(1)}, bf16[8,1536]{1,0:T(8,128)(2,1)S(1)}) custom-call(s32[8,128]{1,0:T(8,128)S(1)} %lane.1.lane_ref, s32[1,48]{1,0:T(1,128)S(1)} %copy-done.2, s32[48]{0:T(128)S(1)} %copy-done.3, bf16[8,6144]{1,0:T(8,128)(2,1)S(1)} %copy-done.1), custom_call_target="tpu_custom_call" | custom-call | tf_op jit(solution)/shard_map/live_blocks/pallas_call | solution.py:19
  6.0 2.7 %collective-permute-start = (bf16[8,1536]{1,0:T(8,128)(2,1)S(1)}, bf16[8,1536]{1,0:T(8,128)(2,1)S(1)}, u32[]{:S(2)}, u32[]{:S(2)}) collective-permute-start(bf16[8,1536]{1,0:T(8,128)(2,1)S(1)} %get-tuple-element.27), channel_id=1, source_target_pairs={{0,4},{1,5},{2,6},{3,7},{4,0},{5,1},{6,2},{7,3},{8,12},{9,13},{10,... | collective-permute-start | bytes 73736 | tf_op jit(solution)/shard_map/ppermute | solution.py:83
  8.7 1.3 %collective-permute-start.2 = (bf16[8,1536]{1,0:T(8,128)(2,1)S(1)}, bf16[8,1536]{1,0:T(8,128)(2,1)S(1)}, u32[]{:S(2)}, u32[]{:S(2)}) collective-permute-start(bf16[8,1536]{1,0:T(8,128)(2,1)S(1)} %get-tuple-element.32), channel_id=1, source_target_pairs={{0,6},{1,7},{2,4},{3,5},{4,2},{5,3},{6,0},{7,1},{8,14},{9,15},{10,... | collective-permute-start | bytes 73736 | tf_op jit(solution)/shard_map/ppermute | solution.py:83
  10.0 0.0 collective-permute-done.1.refs_5_
  10.0 1.1 %collective-permute-start.3 = (bf16[8,1536]{1,0:T(8,128)(2,1)S(1)}, bf16[8,1536]{1,0:T(8,128)(2,1)S(1)}, u32[]{:S(2)}, u32[]{:S(2)}) collective-permute-start(bf16[8,1536]{1,0:T(8,128)(2,1)S(1)} %get-tuple-element.33), channel_id=1, source_target_pairs={{0,2},{1,3},{2,0},{3,1},{4,6},{5,7},{6,4},{7,5},{8,10},{9,11},{10,... | collective-permute-start | bytes 73736 | tf_op jit(solution)/shard_map/ppermute | solution.py:83
  11.1 0.0 collective-permute-done.refs_1_
  11.1 0.0 collective-permute-start.8
  11.1 3.2 %collective-permute-done.2.refs_2_ = bf16[8,1536]{1,0:T(8,128)(2,1)S(1)} collective-permute-done((bf16[8,1536]{1,0:T(8,128)(2,1)S(1)}, bf16[8,1536]{1,0:T(8,128)(2,1)S(1)}, u32[]{:S(2)}, u32[]{:S(2)}) %collective-permute-start.2) | collective-permute-done | bytes 24608 | tf_op jit(solution)/shard_map/ppermute | solution.py:83
  14.3 0.0 collective-permute-start.9
  14.3 0.0 collective-permute-done.4.refs_4_
  14.3 0.0 collective-permute-done.3.refs_3_
  14.3 0.0 collective-permute-done.5.refs_5_
  14.3 0.6 %collective-permute-start.7 = (bf16[768,128]{1,0:T(8,128)(2,1)S(1)}, bf16[768,128]{1,0:T(8,128)(2,1)S(1)}, u32[]{:S(2)}, u32[]{:S(2)}) collective-permute-start(bf16[768,128]{1,0:T(8,128)(2,1)S(1)} %collective-permute-done.5.refs_5_), channel_id=1, source_target_pairs={{0,1},{1,0},{2,3},{3,2},{4,5},{5,4},{6,7},{7,6},{8,9},{9,8},{10,11... | collective-permute-start | bytes 589832 | tf_op jit(solution)/shard_map/ppermute | solution.py:83
  14.9 0.1 collective-permute-start.6
  15.0 0.0 collective-permute-done.8.refs_6_
  15.0 0.8 %collective-permute-done.9.refs_7_ = bf16[768,128]{1,0:T(8,128)(2,1)S(1)} collective-permute-done((bf16[768,128]{1,0:T(8,128)(2,1)S(1)}, bf16[768,128]{1,0:T(8,128)(2,1)S(1)}, u32[]{:S(2)}, u32[]{:S(2)}) %collective-permute-start.9) | collective-permute-done | bytes 196640 | tf_op jit(solution)/shard_map/ppermute | solution.py:83
  15.7 0.2 dots_first.1.refs_8_
  16.0 0.0 collective-permute-done.7.refs_7_
  16.0 0.3 %collective-permute-done.6.refs_6_ = bf16[768,128]{1,0:T(8,128)(2,1)S(1)} collective-permute-done((bf16[768,128]{1,0:T(8,128)(2,1)S(1)}, bf16[768,128]{1,0:T(8,128)(2,1)S(1)}, u32[]{:S(2)}, u32[]{:S(2)}) %collective-permute-start.6) | collective-permute-done | bytes 196640 | tf_op jit(solution)/shard_map/ppermute | solution.py:83
  16.3 0.2 dots_rest.1
  16.6 0.6 %collective-permute-start.10 = (f32[8,512]{1,0:T(8,128)S(1)}, f32[8,512]{1,0:T(8,128)S(1)}, u32[]{:S(2)}, u32[]{:S(2)}) collective-permute-start(f32[8,512]{1,0:T(8,128)S(1)} %get-tuple-element.45), channel_id=1, source_target_pairs={{0,2},{1,3},{2,6},{3,7},{4,0},{5,1},{6,4},{7,5},{8,10},{9,11},{10,... | collective-permute-start | bytes 49160 | tf_op jit(solution)/shard_map/ppermute | solution.py:90
  17.2 2.5 %collective-permute-start.11 = (f32[8,512]{1,0:T(8,128)S(1)}, f32[8,512]{1,0:T(8,128)S(1)}, u32[]{:S(2)}, u32[]{:S(2)}) collective-permute-start(f32[8,512]{1,0:T(8,128)S(1)} %get-tuple-element.47), channel_id=1, source_target_pairs={{0,6},{1,7},{2,4},{3,5},{4,2},{5,3},{6,0},{7,1},{8,14},{9,15},{10,... | collective-permute-start | bytes 49160 | tf_op jit(solution)/shard_map/ppermute | solution.py:90
  19.7 1.6 %collective-permute-start.12 = (f32[8,512]{1,0:T(8,128)S(1)}, f32[8,512]{1,0:T(8,128)S(1)}, u32[]{:S(2)}, u32[]{:S(2)}) collective-permute-start(f32[8,512]{1,0:T(8,128)S(1)} %get-tuple-element.46), channel_id=1, source_target_pairs={{0,4},{1,5},{2,0},{3,1},{4,6},{5,7},{6,2},{7,3},{8,12},{9,13},{10,... | collective-permute-start | bytes 49160 | tf_op jit(solution)/shard_map/ppermute | solution.py:90
  21.3 0.0 collective-permute-done.10
  21.3 1.5 %collective-permute-done.11 = f32[8,512]{1,0:T(8,128)S(1)} collective-permute-done((f32[8,512]{1,0:T(8,128)S(1)}, f32[8,512]{1,0:T(8,128)S(1)}, u32[]{:S(2)}, u32[]{:S(2)}) %collective-permute-start.11) | collective-permute-done | bytes 16416 | tf_op jit(solution)/shard_map/ppermute | solution.py:90
  22.8 0.7 %collective-permute-done.12 = f32[8,512]{1,0:T(8,128)S(1)} collective-permute-done((f32[8,512]{1,0:T(8,128)S(1)}, f32[8,512]{1,0:T(8,128)S(1)}, u32[]{:S(2)}, u32[]{:S(2)}) %collective-permute-start.12) | collective-permute-done | bytes 16416 | tf_op jit(solution)/shard_map/ppermute | solution.py:90
  23.4 0.6 %fusion.2 = bf16[8,512]{1,0:T(8,128)(2,1)} fusion(f32[8,512]{1,0:T(8,128)S(1)} %collective-permute-done.12, f32[8,512]{1,0:T(8,128)S(1)} %collective-permute-done.11, f32[8,512]{1,0:T(8,128)S(1)} %collective-permute-done.10, f32[32,512]{1,0:T(8,128)S(1)} %dots_rest.1), kind=kLoop, calls=%fused_computation.3 | loop fusion | flops 16384 | bytes 73728 | tf_op jit(solution)/shard_map/convert_element_type | solution.py:147
  (2 shorter events, 0.0 us)
Async XLA Ops:
  0.0 3.0 %copy-start = (bf16[768,128]{1,0:T(8,128)(2,1)S(1)}, bf16[768,128]{1,0:T(8,128)(2,1)}, u32[]{:S(2)}) copy-start(bf16[768,128]{1,0:T(8,128)(2,1)} %refs_4_) | copy-start | bytes 589828
  0.0 5.3 %copy-start.1 = (bf16[8,6144]{1,0:T(8,128)(2,1)S(1)}, bf16[8,6144]{1,0:T(8,128)(2,1)}, u32[]{:S(2)}) copy-start(bf16[8,6144]{1,0:T(8,128)(2,1)} %amplitude_ref.1) | copy-start | bytes 294916
  0.0 5.3 %copy-start.2 = (s32[1,48]{1,0:T(1,128)S(1)}, s32[1,48]{1,0:T(1,128)}, u32[]{:S(2)}) copy-start(s32[1,48]{1,0:T(1,128)} %mask_ref.1) | copy-start | bytes 580
  0.0 5.3 %copy-start.3 = (s32[48]{0:T(128)S(1)}, s32[48]{0:T(128)}, u32[]{:S(2)}) copy-start(s32[48]{0:T(128)} %size_ref.1) | copy-start | bytes 580
  0.0 10.0 %collective-permute-start.1 = (bf16[768,128]{1,0:T(8,128)(2,1)}, bf16[768,128]{1,0:T(8,128)(2,1)S(1)}, u32[]{:S(2)}, u32[]{:S(2)}) collective-permute-start(bf16[768,128]{1,0:T(8,128)(2,1)} %refs_4_), channel_id=1, source_target_pairs={{0,8},{8,0},{16,24},{24,16},{1,9},{9,1},{17,25},{25,17},{2,10},{10... | collective-permute-start | bytes 589832 | tf_op jit(solution)/shard_map/ppermute | solution.py:83
  3.0 11.3 %collective-permute-start.4 = (bf16[768,128]{1,0:T(8,128)(2,1)S(1)}, bf16[768,128]{1,0:T(8,128)(2,1)S(1)}, u32[]{:S(2)}, u32[]{:S(2)}) collective-permute-start(bf16[768,128]{1,0:T(8,128)(2,1)S(1)} %copy-done), channel_id=1, source_target_pairs={{0,16},{8,24},{16,0},{24,8},{1,17},{9,25},{17,1},{25,9},{2,18},{10... | collective-permute-start | bytes 589832 | tf_op jit(solution)/shard_map/ppermute | solution.py:83
  4.5 9.8 %collective-permute-start.5 = (bf16[768,128]{1,0:T(8,128)(2,1)S(1)}, bf16[768,128]{1,0:T(8,128)(2,1)S(1)}, u32[]{:S(2)}, u32[]{:S(2)}) collective-permute-start(bf16[768,128]{1,0:T(8,128)(2,1)S(1)} %copy-done), channel_id=1, source_target_pairs={{0,24},{8,16},{16,8},{24,0},{1,25},{9,17},{17,9},{25,1},{2,26},{10... | collective-permute-start | bytes 589832 | tf_op jit(solution)/shard_map/ppermute | solution.py:83
  6.0 5.1 %collective-permute-start = (bf16[8,1536]{1,0:T(8,128)(2,1)S(1)}, bf16[8,1536]{1,0:T(8,128)(2,1)S(1)}, u32[]{:S(2)}, u32[]{:S(2)}) collective-permute-start(bf16[8,1536]{1,0:T(8,128)(2,1)S(1)} %get-tuple-element.27), channel_id=1, source_target_pairs={{0,4},{1,5},{2,6},{3,7},{4,0},{5,1},{6,2},{7,3},{8,12},{9,13},{10,... | collective-permute-start | bytes 73736 | tf_op jit(solution)/shard_map/ppermute | solution.py:83
  8.7 5.6 %collective-permute-start.2 = (bf16[8,1536]{1,0:T(8,128)(2,1)S(1)}, bf16[8,1536]{1,0:T(8,128)(2,1)S(1)}, u32[]{:S(2)}, u32[]{:S(2)}) collective-permute-start(bf16[8,1536]{1,0:T(8,128)(2,1)S(1)} %get-tuple-element.32), channel_id=1, source_target_pairs={{0,6},{1,7},{2,4},{3,5},{4,2},{5,3},{6,0},{7,1},{8,14},{9,15},{10,... | collective-permute-start | bytes 73736 | tf_op jit(solution)/shard_map/ppermute | solution.py:83
  10.0 4.3 %collective-permute-start.3 = (bf16[8,1536]{1,0:T(8,128)(2,1)S(1)}, bf16[8,1536]{1,0:T(8,128)(2,1)S(1)}, u32[]{:S(2)}, u32[]{:S(2)}) collective-permute-start(bf16[8,1536]{1,0:T(8,128)(2,1)S(1)} %get-tuple-element.33), channel_id=1, source_target_pairs={{0,2},{1,3},{2,0},{3,1},{4,6},{5,7},{6,4},{7,5},{8,10},{9,11},{10,... | collective-permute-start | bytes 73736 | tf_op jit(solution)/shard_map/ppermute | solution.py:83
  11.1 3.9 %collective-permute-start.8 = (bf16[768,128]{1,0:T(8,128)(2,1)S(1)}, bf16[768,128]{1,0:T(8,128)(2,1)S(1)}, u32[]{:S(2)}, u32[]{:S(2)}) collective-permute-start(bf16[768,128]{1,0:T(8,128)(2,1)S(1)} %copy-done), channel_id=1, source_target_pairs={{0,1},{1,0},{2,3},{3,2},{4,5},{5,4},{6,7},{7,6},{8,9},{9,8},{10,11... | collective-permute-start | bytes 589832 | tf_op jit(solution)/shard_map/ppermute | solution.py:83
  14.3 1.4 %collective-permute-start.9 = (bf16[768,128]{1,0:T(8,128)(2,1)S(1)}, bf16[768,128]{1,0:T(8,128)(2,1)S(1)}, u32[]{:S(2)}, u32[]{:S(2)}) collective-permute-start(bf16[768,128]{1,0:T(8,128)(2,1)S(1)} %collective-permute-done.1.refs_5_), channel_id=1, source_target_pairs={{0,1},{1,0},{2,3},{3,2},{4,5},{5,4},{6,7},{7,6},{8,9},{9,8},{10,11... | collective-permute-start | bytes 589832 | tf_op jit(solution)/shard_map/ppermute | solution.py:83
  14.3 1.7 %collective-permute-start.7 = (bf16[768,128]{1,0:T(8,128)(2,1)S(1)}, bf16[768,128]{1,0:T(8,128)(2,1)S(1)}, u32[]{:S(2)}, u32[]{:S(2)}) collective-permute-start(bf16[768,128]{1,0:T(8,128)(2,1)S(1)} %collective-permute-done.5.refs_5_), channel_id=1, source_target_pairs={{0,1},{1,0},{2,3},{3,2},{4,5},{5,4},{6,7},{7,6},{8,9},{9,8},{10,11... | collective-permute-start | bytes 589832 | tf_op jit(solution)/shard_map/ppermute | solution.py:83
  14.9 1.4 %collective-permute-start.6 = (bf16[768,128]{1,0:T(8,128)(2,1)S(1)}, bf16[768,128]{1,0:T(8,128)(2,1)S(1)}, u32[]{:S(2)}, u32[]{:S(2)}) collective-permute-start(bf16[768,128]{1,0:T(8,128)(2,1)S(1)} %collective-permute-done.4.refs_4_), channel_id=1, source_target_pairs={{0,1},{1,0},{2,3},{3,2},{4,5},{5,4},{6,7},{7,6},{8,9},{9,8},{10,11... | collective-permute-start | bytes 589832 | tf_op jit(solution)/shard_map/ppermute | solution.py:83
  16.6 4.7 %collective-permute-start.10 = (f32[8,512]{1,0:T(8,128)S(1)}, f32[8,512]{1,0:T(8,128)S(1)}, u32[]{:S(2)}, u32[]{:S(2)}) collective-permute-start(f32[8,512]{1,0:T(8,128)S(1)} %get-tuple-element.45), channel_id=1, source_target_pairs={{0,2},{1,3},{2,6},{3,7},{4,0},{5,1},{6,4},{7,5},{8,10},{9,11},{10,... | collective-permute-start | bytes 49160 | tf_op jit(solution)/shard_map/ppermute | solution.py:90
  17.2 5.5 %collective-permute-start.11 = (f32[8,512]{1,0:T(8,128)S(1)}, f32[8,512]{1,0:T(8,128)S(1)}, u32[]{:S(2)}, u32[]{:S(2)}) collective-permute-start(f32[8,512]{1,0:T(8,128)S(1)} %get-tuple-element.47), channel_id=1, source_target_pairs={{0,6},{1,7},{2,4},{3,5},{4,2},{5,3},{6,0},{7,1},{8,14},{9,15},{10,... | collective-permute-start | bytes 49160 | tf_op jit(solution)/shard_map/ppermute | solution.py:90
  19.7 3.7 %collective-permute-start.12 = (f32[8,512]{1,0:T(8,128)S(1)}, f32[8,512]{1,0:T(8,128)S(1)}, u32[]{:S(2)}, u32[]{:S(2)}) collective-permute-start(f32[8,512]{1,0:T(8,128)S(1)} %get-tuple-element.46), channel_id=1, source_target_pairs={{0,4},{1,5},{2,0},{3,1},{4,6},{5,7},{6,2},{7,3},{8,12},{9,13},{10,... | collective-permute-start | bytes 49160 | tf_op jit(solution)/shard_map/ppermute | solution.py:90

commit v6 on v4

--- a/solution.py
+++ b/solution.py
@@ -48,16 +48,25 @@
                 out_ref[:, place : place + tile] = jnp.where(lane < live, value, jnp.zeros_like(value))
 
 
-def dot_kernel(members, blocks, *refs):
-    live_refs, own_refs, other_refs = refs[:members], refs[members : members + blocks], refs[members + blocks : -1]
+def dot_kernel(members, first, blocks, early, *refs):
+    live_refs, own_refs, other_refs = refs[:members], refs[members : members + blocks], refs[members + blocks :][:blocks]
     out_ref = refs[-1]
     blk = lax.axis_index("blk")
     depth, cols = own_refs[0].shape
     live = jnp.concatenate([ref[...] for ref in live_refs], axis=0)
-    for step, (own_ref, other_ref) in enumerate(zip(own_refs, other_refs)):
+    done = 0
+    for ref in () if early else refs[members + 2 * blocks : -1]:
+        for k in range(ref.shape[1] // cols):
+            place = pl.ds(pl.multiple_of((blk ^ done) * cols, cols), cols)
+            out_ref[:, place] = ref[:, k * cols : (k + 1) * cols]
+            done += 1
+    for step, (own_ref, other_ref) in enumerate(zip(own_refs, other_refs), first):
         total = jnp.dot(live[:, :depth], own_ref[...], preferred_element_type=jnp.float32)
         total += jnp.dot(live[:, depth:], other_ref[...], preferred_element_type=jnp.float32)
-        out_ref[:, pl.ds(pl.multiple_of((blk ^ step) * cols, cols), cols)] = total
+        if early:
+            out_ref[:, (step - first) * cols : (step - first + 1) * cols] = total
+        else:
+            out_ref[:, pl.ds(pl.multiple_of((blk ^ step) * cols, cols), cols)] = total
 
 
 def after(received, places, value):
@@ -115,13 +124,21 @@
         own[step] = after(received, places, own[step])
         other.append(swap(own[step], "grp", grp_size, 1))
 
-    partial = local_call(
-        functools.partial(dot_kernel, chips, blk_size),
-        "dots",
-        jax.ShapeDtypeStruct((chips * rows, blk_size * cols), jnp.float32),
-        [VMEM] * (chips + 2 * blk_size),
-        [*received, *own, *other],
-    )
+    shape = lambda count: jax.ShapeDtypeStruct((chips * rows, count * cols), jnp.float32)
+    cuts = [0, blk_size // 2, blk_size - 1, blk_size]
+    heads = []
+    for low, high in zip(cuts[:-1], cuts[1:]):
+        last = high == blk_size
+        heads.append(
+            local_call(
+                functools.partial(dot_kernel, chips, low, high - low, not last),
+                f"dots_{low}",
+                shape(blk_size if last else high - low),
+                [VMEM] * (chips + 2 * (high - low) + len(heads) * last),
+                [*received, *own[low:high], *other[low:high], *(heads if last else [])],
+            )
+        )
+    partial = heads[-1]
     ladder = partial[:rows]
     for step in range(1, chips):
         place = 0

time: 24.3 us -> 24.1 us (level)
  waiting for transfers between devices: 6.73 us -> 6.3 us
  Pallas kernels: 1.02 us -> 1.27 us
    ppermute x10, waiting for transfers between devices: 4.56 us -> 4.14 us  [swap(): return lax.ppermute(array, axis, [(k, k ^ step) for k in range(size)])]
    pallas_call x3 -> x5, Pallas kernels: 1.02 us -> 1.27 us  [local_call(): pl.pallas_call(kernel, out_shape=out_shape, in_specs=in_specs, out_specs=...]
  transfers between devices with their start and end apart: 13 -> 13, of which waited for: 6 -> 5; matrix products, arithmetic and copies ran while one was open for 0% -> 0% of each run, Pallas kernels for 3% -> 5%
where the time goes in v6:
time: 24.1 us; the launch traced here: 24 us
  starting transfers between devices  15.7 us (65%)
  waiting for transfers between devices  6.3 us (26%)
  Pallas kernels  1.27 us (5%)
  other arithmetic  0.61 us (3%)
    ppermute x10, starting transfers between devices, swap(): return lax.ppermute(array, axis, [(k, k ^ step) for k in range(size)])  11 us
    ppermute x3, starting transfers between devices, shift(): return lax.ppermute(array, 'grp', pairs)  4.67 us
    ppermute x10, waiting for transfers between devices, swap(): return lax.ppermute(array, axis, [(k, k ^ step) for k in range(size)])  4.14 us
    ppermute x3, waiting for transfers between devices, shift(): return lax.ppermute(array, 'grp', pairs)  2.16 us
    pallas_call x5, Pallas kernels, local_call(): pl.pallas_call(kernel, out_shape=out_shape, in_specs=in_specs, out_specs=...  1.27 us
    convert_element_type x1, other arithmetic, body(): return ladder.astype(jnp.bfloat16)  0.61 us
  transfers between devices with their start and end apart: 13, of which 5 were waited for; matrix products, arithmetic and copies ran while one was open for 0% of the time, Pallas kernels for 5%

profile of v6, /device:TPU:0, one launch (start us, length us, event | category | flops | bytes accessed | tf_op | source)
XLA Modules:
  0.0 24.0 jit_solution(5301839316282467566)
XLA Ops:
  0.0 0.0 copy-start
  0.0 0.0 copy-start.1
  0.0 0.0 copy-start.2
  0.0 0.0 copy-start.3
  0.0 3.0 %collective-permute-start.1 = (bf16[768,128]{1,0:T(8,128)(2,1)}, bf16[768,128]{1,0:T(8,128)(2,1)S(1)}, u32[]{:S(2)}, u32[]{:S(2)}) collective-permute-start(bf16[768,128]{1,0:T(8,128)(2,1)} %refs_4_), channel_id=1, source_target_pairs={{0,8},{8,0},{16,24},{24,16},{1,9},{9,1},{17,25},{25,17},{2,10},{10... | collective-permute-start | bytes 589832 | tf_op jit(solution)/shard_map/ppermute | solution.py:86
  3.0 0.0 copy-done
  3.0 1.5 %collective-permute-start.4 = (bf16[768,128]{1,0:T(8,128)(2,1)S(1)}, bf16[768,128]{1,0:T(8,128)(2,1)S(1)}, u32[]{:S(2)}, u32[]{:S(2)}) collective-permute-start(bf16[768,128]{1,0:T(8,128)(2,1)S(1)} %copy-done), channel_id=1, source_target_pairs={{0,16},{8,24},{16,0},{24,8},{1,17},{9,25},{17,1},{25,9},{2,18},{10... | collective-permute-start | bytes 589832 | tf_op jit(solution)/shard_map/ppermute | solution.py:86
  4.5 0.8 %collective-permute-start.5 = (bf16[768,128]{1,0:T(8,128)(2,1)S(1)}, bf16[768,128]{1,0:T(8,128)(2,1)S(1)}, u32[]{:S(2)}, u32[]{:S(2)}) collective-permute-start(bf16[768,128]{1,0:T(8,128)(2,1)S(1)} %copy-done), channel_id=1, source_target_pairs={{0,24},{8,16},{16,8},{24,0},{1,25},{9,17},{17,9},{25,1},{2,26},{10... | collective-permute-start | bytes 589832 | tf_op jit(solution)/shard_map/ppermute | solution.py:86
  5.3 0.0 copy-done.1
  5.3 0.0 copy-done.2
  5.3 0.0 copy-done.3
  5.3 0.7 %live_blocks.1 = (bf16[8,1536]{1,0:T(8,128)(2,1)S(1)}, bf16[8,1536]{1,0:T(8,128)(2,1)S(1)}, bf16[8,1536]{1,0:T(8,128)(2,1)S(1)}, bf16[8,1536]{1,0:T(8,128)(2,1)S(1)}) custom-call(s32[8,128]{1,0:T(8,128)S(1)} %lane.1.lane_ref, s32[1,48]{1,0:T(1,128)S(1)} %copy-done.2, s32[48]{0:T(128)S(1)} %copy-done.3, bf16[8,6144]{1,0:T(8,128)(2,1)S(1)} %copy-done.1), custom_call_target="tpu_custom_call" | custom-call | tf_op jit(solution)/shard_map/live_blocks/pallas_call | solution.py:19
  6.0 2.7 %collective-permute-start = (bf16[8,1536]{1,0:T(8,128)(2,1)S(1)}, bf16[8,1536]{1,0:T(8,128)(2,1)S(1)}, u32[]{:S(2)}, u32[]{:S(2)}) collective-permute-start(bf16[8,1536]{1,0:T(8,128)(2,1)S(1)} %get-tuple-element.27), channel_id=1, source_target_pairs={{0,4},{1,5},{2,6},{3,7},{4,0},{5,1},{6,2},{7,3},{8,12},{9,13},{10,... | collective-permute-start | bytes 73736 | tf_op jit(solution)/shard_map/ppermute | solution.py:86
  8.7 1.3 %collective-permute-start.2 = (bf16[8,1536]{1,0:T(8,128)(2,1)S(1)}, bf16[8,1536]{1,0:T(8,128)(2,1)S(1)}, u32[]{:S(2)}, u32[]{:S(2)}) collective-permute-start(bf16[8,1536]{1,0:T(8,128)(2,1)S(1)} %get-tuple-element.32), channel_id=1, source_target_pairs={{0,6},{1,7},{2,4},{3,5},{4,2},{5,3},{6,0},{7,1},{8,14},{9,15},{10,... | collective-permute-start | bytes 73736 | tf_op jit(solution)/shard_map/ppermute | solution.py:86
  10.0 0.0 collective-permute-done.1.refs_5_
  10.0 1.1 %collective-permute-start.3 = (bf16[8,1536]{1,0:T(8,128)(2,1)S(1)}, bf16[8,1536]{1,0:T(8,128)(2,1)S(1)}, u32[]{:S(2)}, u32[]{:S(2)}) collective-permute-start(bf16[8,1536]{1,0:T(8,128)(2,1)S(1)} %get-tuple-element.33), channel_id=1, source_target_pairs={{0,2},{1,3},{2,0},{3,1},{4,6},{5,7},{6,4},{7,5},{8,10},{9,11},{10,... | collective-permute-start | bytes 73736 | tf_op jit(solution)/shard_map/ppermute | solution.py:86
  11.1 0.0 collective-permute-done.refs_1_
  11.1 0.0 collective-permute-start.7
  11.1 3.2 %collective-permute-done.2.refs_2_ = bf16[8,1536]{1,0:T(8,128)(2,1)S(1)} collective-permute-done((bf16[8,1536]{1,0:T(8,128)(2,1)S(1)}, bf16[8,1536]{1,0:T(8,128)(2,1)S(1)}, u32[]{:S(2)}, u32[]{:S(2)}) %collective-permute-start.2) | collective-permute-done | bytes 24608 | tf_op jit(solution)/shard_map/ppermute | solution.py:86
  14.3 0.0 collective-permute-start.8
  14.3 0.0 collective-permute-done.4.refs_4_
  14.3 0.0 collective-permute-done.3.refs_3_
  14.3 0.0 collective-permute-done.5.refs_4_
  14.3 0.6 %collective-permute-start.9 = (bf16[768,128]{1,0:T(8,128)(2,1)S(1)}, bf16[768,128]{1,0:T(8,128)(2,1)S(1)}, u32[]{:S(2)}, u32[]{:S(2)}) collective-permute-start(bf16[768,128]{1,0:T(8,128)(2,1)S(1)} %collective-permute-done.4.refs_4_), channel_id=1, source_target_pairs={{0,1},{1,0},{2,3},{3,2},{4,5},{5,4},{6,7},{7,6},{8,9},{9,8},{10,11... | collective-permute-start | bytes 589832 | tf_op jit(solution)/shard_map/ppermute | solution.py:86
  14.9 0.1 collective-permute-start.6
  15.0 0.0 collective-permute-done.7.refs_6_
  15.0 0.8 %collective-permute-done.8.refs_7_ = bf16[768,128]{1,0:T(8,128)(2,1)S(1)} collective-permute-done((bf16[768,128]{1,0:T(8,128)(2,1)S(1)}, bf16[768,128]{1,0:T(8,128)(2,1)S(1)}, u32[]{:S(2)}, u32[]{:S(2)}) %collective-permute-start.8) | collective-permute-done | bytes 196640 | tf_op jit(solution)/shard_map/ppermute | solution.py:86
  15.7 0.2 dots_0.1.refs_6_
  16.0 0.0 collective-permute-done.9.refs_5_
  16.0 0.2 dots_2.1.refs_7_
  16.2 0.1 collective-permute-done.6.refs_5_
  16.3 0.2 dots_3.1
  16.5 0.6 %collective-permute-start.10 = (f32[8,512]{1,0:T(8,128)S(1)}, f32[8,512]{1,0:T(8,128)S(1)}, u32[]{:S(2)}, u32[]{:S(2)}) collective-permute-start(f32[8,512]{1,0:T(8,128)S(1)} %get-tuple-element.45), channel_id=1, source_target_pairs={{0,2},{1,3},{2,6},{3,7},{4,0},{5,1},{6,4},{7,5},{8,10},{9,11},{10,... | collective-permute-start | bytes 49160 | tf_op jit(solution)/shard_map/ppermute | solution.py:93
  17.2 2.5 %collective-permute-start.11 = (f32[8,512]{1,0:T(8,128)S(1)}, f32[8,512]{1,0:T(8,128)S(1)}, u32[]{:S(2)}, u32[]{:S(2)}) collective-permute-start(f32[8,512]{1,0:T(8,128)S(1)} %get-tuple-element.47), channel_id=1, source_target_pairs={{0,6},{1,7},{2,4},{3,5},{4,2},{5,3},{6,0},{7,1},{8,14},{9,15},{10,... | collective-permute-start | bytes 49160 | tf_op jit(solution)/shard_map/ppermute | solution.py:93
  19.6 1.6 %collective-permute-start.12 = (f32[8,512]{1,0:T(8,128)S(1)}, f32[8,512]{1,0:T(8,128)S(1)}, u32[]{:S(2)}, u32[]{:S(2)}) collective-permute-start(f32[8,512]{1,0:T(8,128)S(1)} %get-tuple-element.46), channel_id=1, source_target_pairs={{0,4},{1,5},{2,0},{3,1},{4,6},{5,7},{6,2},{7,3},{8,12},{9,13},{10,... | collective-permute-start | bytes 49160 | tf_op jit(solution)/shard_map/ppermute | solution.py:93
  21.2 0.0 collective-permute-done.10
  21.2 1.5 %collective-permute-done.11 = f32[8,512]{1,0:T(8,128)S(1)} collective-permute-done((f32[8,512]{1,0:T(8,128)S(1)}, f32[8,512]{1,0:T(8,128)S(1)}, u32[]{:S(2)}, u32[]{:S(2)}) %collective-permute-start.11) | collective-permute-done | bytes 16416 | tf_op jit(solution)/shard_map/ppermute | solution.py:93
  22.7 0.7 %collective-permute-done.12 = f32[8,512]{1,0:T(8,128)S(1)} collective-permute-done((f32[8,512]{1,0:T(8,128)S(1)}, f32[8,512]{1,0:T(8,128)S(1)}, u32[]{:S(2)}, u32[]{:S(2)}) %collective-permute-start.12) | collective-permute-done | bytes 16416 | tf_op jit(solution)/shard_map/ppermute | solution.py:93
  23.4 0.6 %fusion.2 = bf16[8,512]{1,0:T(8,128)(2,1)} fusion(f32[8,512]{1,0:T(8,128)S(1)} %collective-permute-done.12, f32[8,512]{1,0:T(8,128)S(1)} %collective-permute-done.11, f32[8,512]{1,0:T(8,128)S(1)} %collective-permute-done.10, f32[32,512]{1,0:T(8,128)S(1)} %dots_3.1), kind=kLoop, calls=%fused_computation.3 | loop fusion | flops 16384 | bytes 73728 | tf_op jit(solution)/shard_map/convert_element_type | solution.py:148
  (2 shorter events, 0.0 us)
Async XLA Ops:
  0.0 3.0 %copy-start = (bf16[768,128]{1,0:T(8,128)(2,1)S(1)}, bf16[768,128]{1,0:T(8,128)(2,1)}, u32[]{:S(2)}) copy-start(bf16[768,128]{1,0:T(8,128)(2,1)} %refs_4_) | copy-start | bytes 589828
  0.0 5.3 %copy-start.1 = (bf16[8,6144]{1,0:T(8,128)(2,1)S(1)}, bf16[8,6144]{1,0:T(8,128)(2,1)}, u32[]{:S(2)}) copy-start(bf16[8,6144]{1,0:T(8,128)(2,1)} %amplitude_ref.1) | copy-start | bytes 294916
  0.0 5.3 %copy-start.2 = (s32[1,48]{1,0:T(1,128)S(1)}, s32[1,48]{1,0:T(1,128)}, u32[]{:S(2)}) copy-start(s32[1,48]{1,0:T(1,128)} %mask_ref.1) | copy-start | bytes 580
  0.0 5.3 %copy-start.3 = (s32[48]{0:T(128)S(1)}, s32[48]{0:T(128)}, u32[]{:S(2)}) copy-start(s32[48]{0:T(128)} %size_ref.1) | copy-start | bytes 580
  0.0 10.0 %collective-permute-start.1 = (bf16[768,128]{1,0:T(8,128)(2,1)}, bf16[768,128]{1,0:T(8,128)(2,1)S(1)}, u32[]{:S(2)}, u32[]{:S(2)}) collective-permute-start(bf16[768,128]{1,0:T(8,128)(2,1)} %refs_4_), channel_id=1, source_target_pairs={{0,8},{8,0},{16,24},{24,16},{1,9},{9,1},{17,25},{25,17},{2,10},{10... | collective-permute-start | bytes 589832 | tf_op jit(solution)/shard_map/ppermute | solution.py:86
  3.0 11.3 %collective-permute-start.4 = (bf16[768,128]{1,0:T(8,128)(2,1)S(1)}, bf16[768,128]{1,0:T(8,128)(2,1)S(1)}, u32[]{:S(2)}, u32[]{:S(2)}) collective-permute-start(bf16[768,128]{1,0:T(8,128)(2,1)S(1)} %copy-done), channel_id=1, source_target_pairs={{0,16},{8,24},{16,0},{24,8},{1,17},{9,25},{17,1},{25,9},{2,18},{10... | collective-permute-start | bytes 589832 | tf_op jit(solution)/shard_map/ppermute | solution.py:86
  4.5 9.8 %collective-permute-start.5 = (bf16[768,128]{1,0:T(8,128)(2,1)S(1)}, bf16[768,128]{1,0:T(8,128)(2,1)S(1)}, u32[]{:S(2)}, u32[]{:S(2)}) collective-permute-start(bf16[768,128]{1,0:T(8,128)(2,1)S(1)} %copy-done), channel_id=1, source_target_pairs={{0,24},{8,16},{16,8},{24,0},{1,25},{9,17},{17,9},{25,1},{2,26},{10... | collective-permute-start | bytes 589832 | tf_op jit(solution)/shard_map/ppermute | solution.py:86
  6.0 5.1 %collective-permute-start = (bf16[8,1536]{1,0:T(8,128)(2,1)S(1)}, bf16[8,1536]{1,0:T(8,128)(2,1)S(1)}, u32[]{:S(2)}, u32[]{:S(2)}) collective-permute-start(bf16[8,1536]{1,0:T(8,128)(2,1)S(1)} %get-tuple-element.27), channel_id=1, source_target_pairs={{0,4},{1,5},{2,6},{3,7},{4,0},{5,1},{6,2},{7,3},{8,12},{9,13},{10,... | collective-permute-start | bytes 73736 | tf_op jit(solution)/shard_map/ppermute | solution.py:86
  8.7 5.6 %collective-permute-start.2 = (bf16[8,1536]{1,0:T(8,128)(2,1)S(1)}, bf16[8,1536]{1,0:T(8,128)(2,1)S(1)}, u32[]{:S(2)}, u32[]{:S(2)}) collective-permute-start(bf16[8,1536]{1,0:T(8,128)(2,1)S(1)} %get-tuple-element.32), channel_id=1, source_target_pairs={{0,6},{1,7},{2,4},{3,5},{4,2},{5,3},{6,0},{7,1},{8,14},{9,15},{10,... | collective-permute-start | bytes 73736 | tf_op jit(solution)/shard_map/ppermute | solution.py:86
  10.0 4.3 %collective-permute-start.3 = (bf16[8,1536]{1,0:T(8,128)(2,1)S(1)}, bf16[8,1536]{1,0:T(8,128)(2,1)S(1)}, u32[]{:S(2)}, u32[]{:S(2)}) collective-permute-start(bf16[8,1536]{1,0:T(8,128)(2,1)S(1)} %get-tuple-element.33), channel_id=1, source_target_pairs={{0,2},{1,3},{2,0},{3,1},{4,6},{5,7},{6,4},{7,5},{8,10},{9,11},{10,... | collective-permute-start | bytes 73736 | tf_op jit(solution)/shard_map/ppermute | solution.py:86
  11.1 3.9 %collective-permute-start.7 = (bf16[768,128]{1,0:T(8,128)(2,1)S(1)}, bf16[768,128]{1,0:T(8,128)(2,1)S(1)}, u32[]{:S(2)}, u32[]{:S(2)}) collective-permute-start(bf16[768,128]{1,0:T(8,128)(2,1)S(1)} %copy-done), channel_id=1, source_target_pairs={{0,1},{1,0},{2,3},{3,2},{4,5},{5,4},{6,7},{7,6},{8,9},{9,8},{10,11... | collective-permute-start | bytes 589832 | tf_op jit(solution)/shard_map/ppermute | solution.py:86
  14.3 1.4 %collective-permute-start.8 = (bf16[768,128]{1,0:T(8,128)(2,1)S(1)}, bf16[768,128]{1,0:T(8,128)(2,1)S(1)}, u32[]{:S(2)}, u32[]{:S(2)}) collective-permute-start(bf16[768,128]{1,0:T(8,128)(2,1)S(1)} %collective-permute-done.1.refs_5_), channel_id=1, source_target_pairs={{0,1},{1,0},{2,3},{3,2},{4,5},{5,4},{6,7},{7,6},{8,9},{9,8},{10,11... | collective-permute-start | bytes 589832 | tf_op jit(solution)/shard_map/ppermute | solution.py:86
  14.3 1.7 %collective-permute-start.9 = (bf16[768,128]{1,0:T(8,128)(2,1)S(1)}, bf16[768,128]{1,0:T(8,128)(2,1)S(1)}, u32[]{:S(2)}, u32[]{:S(2)}) collective-permute-start(bf16[768,128]{1,0:T(8,128)(2,1)S(1)} %collective-permute-done.4.refs_4_), channel_id=1, source_target_pairs={{0,1},{1,0},{2,3},{3,2},{4,5},{5,4},{6,7},{7,6},{8,9},{9,8},{10,11... | collective-permute-start | bytes 589832 | tf_op jit(solution)/shard_map/ppermute | solution.py:86
  14.9 1.4 %collective-permute-start.6 = (bf16[768,128]{1,0:T(8,128)(2,1)S(1)}, bf16[768,128]{1,0:T(8,128)(2,1)S(1)}, u32[]{:S(2)}, u32[]{:S(2)}) collective-permute-start(bf16[768,128]{1,0:T(8,128)(2,1)S(1)} %collective-permute-done.5.refs_4_), channel_id=1, source_target_pairs={{0,1},{1,0},{2,3},{3,2},{4,5},{5,4},{6,7},{7,6},{8,9},{9,8},{10,11... | collective-permute-start | bytes 589832 | tf_op jit(solution)/shard_map/ppermute | solution.py:86
  16.5 4.7 %collective-permute-start.10 = (f32[8,512]{1,0:T(8,128)S(1)}, f32[8,512]{1,0:T(8,128)S(1)}, u32[]{:S(2)}, u32[]{:S(2)}) collective-permute-start(f32[8,512]{1,0:T(8,128)S(1)} %get-tuple-element.45), channel_id=1, source_target_pairs={{0,2},{1,3},{2,6},{3,7},{4,0},{5,1},{6,4},{7,5},{8,10},{9,11},{10,... | collective-permute-start | bytes 49160 | tf_op jit(solution)/shard_map/ppermute | solution.py:93
  17.2 5.5 %collective-permute-start.11 = (f32[8,512]{1,0:T(8,128)S(1)}, f32[8,512]{1,0:T(8,128)S(1)}, u32[]{:S(2)}, u32[]{:S(2)}) collective-permute-start(f32[8,512]{1,0:T(8,128)S(1)} %get-tuple-element.47), channel_id=1, source_target_pairs={{0,6},{1,7},{2,4},{3,5},{4,2},{5,3},{6,0},{7,1},{8,14},{9,15},{10,... | collective-permute-start | bytes 49160 | tf_op jit(solution)/shard_map/ppermute | solution.py:93
  19.6 3.7 %collective-permute-start.12 = (f32[8,512]{1,0:T(8,128)S(1)}, f32[8,512]{1,0:T(8,128)S(1)}, u32[]{:S(2)}, u32[]{:S(2)}) collective-permute-start(f32[8,512]{1,0:T(8,128)S(1)} %get-tuple-element.46), channel_id=1, source_target_pairs={{0,4},{1,5},{2,0},{3,1},{4,6},{5,7},{6,2},{7,3},{8,12},{9,13},{10,... | collective-permute-start | bytes 49160 | tf_op jit(solution)/shard_map/ppermute | solution.py:93
